TPU v7x, 32 devices: a whole 2x2x4 slice. The times are simulated.
32 devices in a mesh: dp: 2 (over x), seq: 16 (over z, y, core).
Axes of the slice: x: 2, y: 2, z: 4, core: 2. Of those that a mesh axis runs over, the one named last changes fastest.
Arguments:
- inputs: bfloat16 [2, 2, 1024, 1152], P(None, 'dp', 'seq'), may hold values from -8 to 8
- segments: int32 [2, 2, 1024], P(None, 'dp', 'seq'), may hold values from 0 to 9, as said below
- weight_query: bfloat16 [1152, 1152], P('seq', 'dp'), may hold values from -0.1875 to 0.1875
- key_weight_matrix: bfloat16 [1152, 384], P('seq', 'dp'), may hold values from -0.1875 to 0.1875
- value_weight_matrix: bfloat16 [1152, 384], P('seq', 'dp'), may hold values from -0.1875 to 0.1875
- weight_out: bfloat16 [1152, 1152], P('seq', 'dp'), may hold values from -0.75 to 0.75
- weight_gate: bfloat16 [1152, 3072], P('seq', 'dp'), may hold values from -0.1875 to 0.1875
- weight_up: bfloat16 [1152, 3072], P('seq', 'dp'), may hold values from -0.1875 to 0.1875
- weight_down: bfloat16 [3072, 1152], P('seq', 'dp'), may hold values from -0.109375 to 0.109375
- gain_attention: bfloat16 [1152], P('seq'), may hold values from 0.25 to 1.75
- gain_feed: bfloat16 [1152], P('seq'), may hold values from 0.25 to 1.75
- cotangent: bfloat16 [2, 2, 1024, 1152], P(None, 'dp', 'seq'), may hold values from -6 to 6
Outputs:
- output: bfloat16 [2, 2, 1024, 1152], P(None, 'dp', 'seq')
- grad_inputs: bfloat16 [2, 2, 1024, 1152], P(None, 'dp', 'seq')
- grad_query: float32 [1152, 1152], P('seq', 'dp')
- grad_key: float32 [1152, 384], P('seq', 'dp')
- grad_value: float32 [1152, 384], P('seq', 'dp')
- grad_out: float32 [1152, 1152], P('seq', 'dp')
- grad_gate: float32 [1152, 3072], P('seq', 'dp')
- grad_up: float32 [1152, 3072], P('seq', 'dp')
- grad_down: float32 [3072, 1152], P('seq', 'dp')
- grad_gain_attention: float32 [1152], P('seq')
- grad_gain_feed: float32 [1152], P('seq')
- root_means: float32 [3], replicated
Inputs may be any that keep to these rules, and one draw needn't show every extreme that they name: `segments`: within a sequence the numbers never fall; 0 marks padding, which only ends a sequence; for every index of dp, one of its 2 sequences over all micro-batches, drawn from the seed, is a single document that ends within the last 64 positions.
All inputs are finite; a program needn't handle non-finite values.
Results may differ from a plain program's by a relative error of at most 0.015.
Values may be sent and summed in bfloat16 or wider, within the bound.
A program may use at most 256 MiB of HBM per device.

v0:
```python
import math

import jax
import jax.numpy as jnp
from jax import lax
from jax.sharding import PartitionSpec as P

QUERY_HEADS = 18
KEY_VALUE_HEADS = 6
HEAD_DIMENSION = 64


EPS = 1e-05
THETA = 10000.0
NEGATIVE = -1e30


def rope_tables(positions, head_size):
    half_size = head_size // 2
    frequency = THETA ** (-jnp.arange(half_size, dtype=jnp.float32) * 2.0 / head_size)
    angles = positions.astype(jnp.float32)[:, None] * frequency[None, :]
    angles = jnp.concatenate([angles, angles], axis=1)
    return (jnp.cos(angles), jnp.sin(angles))


def turn_half(values_in):
    half_size = values_in.shape[-1] // 2
    return jnp.concatenate([-values_in[..., half_size:], values_in[..., :half_size]], axis=-1)


def apply_rotation(values_in, cosine_table, sine_values):
    return values_in * cosine_table[:, None, :] + turn_half(values_in) * sine_values[:, None, :]


def reverse_rotation(grads_in, cosine_table, sine_values):
    return grads_in * cosine_table[:, None, :] - turn_half(grads_in * sine_values[:, None, :])


def norm_forward(values_in, gain):
    row_scale = lax.rsqrt(jnp.mean(values_in * values_in, axis=-1, keepdims=True) + EPS)
    return (values_in * row_scale * gain, row_scale)


def norm_backward(values_in, row_scale, gain, grad_normed):
    scaled = grad_normed * gain
    inner_mean = jnp.mean(scaled * values_in, axis=-1, keepdims=True)
    value_gradient_rows = row_scale * scaled - values_in * row_scale**3 * inner_mean
    grad_gain = jnp.sum(grad_normed * values_in * row_scale, axis=(0, 1))
    return (value_gradient_rows, grad_gain)


def apply_projection(acts_low, weight_full):
    return jnp.einsum("std,df->stf", acts_low, weight_full, preferred_element_type=jnp.float32)


def project_back(grads_low, weight_full):
    return jnp.einsum("sta,ba->stb", grads_low, weight_full, preferred_element_type=jnp.float32)


def weight_grad(acts_low, grads_low):
    return jnp.einsum("std,stf->df", acts_low, grads_low, preferred_element_type=jnp.float32)


def gather_all(shards, gain_shards):
    wide = (
        lax.all_gather(shards[0], "dp", axis=1, tiled=True),
        lax.all_gather(shards[1], "dp", axis=1, tiled=True),
        lax.all_gather(shards[2], "dp", axis=1, tiled=True),
        lax.all_gather(shards[3], "dp", axis=1, tiled=True),
        lax.all_gather(shards[4], "dp", axis=1, tiled=True),
        lax.all_gather(shards[5], "dp", axis=1, tiled=True),
        lax.all_gather(shards[6], "dp", axis=1, tiled=True),
    )
    return (
        lax.all_gather(wide[0], "seq", axis=0, tiled=True),
        lax.all_gather(wide[1], "seq", axis=0, tiled=True),
        lax.all_gather(wide[2], "seq", axis=0, tiled=True),
        lax.all_gather(wide[3], "seq", axis=0, tiled=True),
        lax.all_gather(wide[4], "seq", axis=0, tiled=True),
        lax.all_gather(wide[5], "seq", axis=0, tiled=True),
        lax.all_gather(wide[6], "seq", axis=0, tiled=True),
        lax.all_gather(gain_shards[0], "seq", axis=0, tiled=True),
        lax.all_gather(gain_shards[1], "seq", axis=0, tiled=True),
    )


def gather_keys(key_low, value_low, seg_low):
    return (
        lax.all_gather(key_low, "seq", axis=1, tiled=True),
        lax.all_gather(value_low, "seq", axis=1, tiled=True),
        lax.all_gather(seg_low, "seq", axis=1, tiled=True),
    )


def reduce_grads(grads):
    seq_count = lax.axis_size("seq")
    flat = [grad_item.reshape(seq_count, -1) for grad_item in grads]
    row_parts = (
        lax.psum_scatter(flat[0], "seq", scatter_dimension=0, tiled=True),
        lax.psum_scatter(flat[1], "seq", scatter_dimension=0, tiled=True),
        lax.psum_scatter(flat[2], "seq", scatter_dimension=0, tiled=True),
        lax.psum_scatter(flat[3], "seq", scatter_dimension=0, tiled=True),
        lax.psum_scatter(flat[4], "seq", scatter_dimension=0, tiled=True),
        lax.psum_scatter(flat[5], "seq", scatter_dimension=0, tiled=True),
        lax.psum_scatter(flat[6], "seq", scatter_dimension=0, tiled=True),
    )
    pieces = [
        part_item.reshape(grad_item.shape[0] // seq_count, grad_item.shape[1])
        for part_item, grad_item in zip(row_parts, grads)
    ]
    return (
        lax.psum_scatter(
            pieces[0].astype(jnp.bfloat16), "dp", scatter_dimension=1, tiled=True
        ).astype(jnp.float32),
        lax.psum_scatter(
            pieces[1].astype(jnp.bfloat16), "dp", scatter_dimension=1, tiled=True
        ).astype(jnp.float32),
        lax.psum_scatter(
            pieces[2].astype(jnp.bfloat16), "dp", scatter_dimension=1, tiled=True
        ).astype(jnp.float32),
        lax.psum_scatter(
            pieces[3].astype(jnp.bfloat16), "dp", scatter_dimension=1, tiled=True
        ).astype(jnp.float32),
        lax.psum_scatter(
            pieces[4].astype(jnp.bfloat16), "dp", scatter_dimension=1, tiled=True
        ).astype(jnp.float32),
        lax.psum_scatter(
            pieces[5].astype(jnp.bfloat16), "dp", scatter_dimension=1, tiled=True
        ).astype(jnp.float32),
        lax.psum_scatter(
            pieces[6].astype(jnp.bfloat16), "dp", scatter_dimension=1, tiled=True
        ).astype(jnp.float32),
    )


def block_view(gathered, block_index, key_tile_block):
    block_offset = block_index * key_tile_block
    key_portion = lax.dynamic_slice_in_dim(gathered[0], block_offset, key_tile_block, 1)
    value_portion = lax.dynamic_slice_in_dim(gathered[1], block_offset, key_tile_block, 1)
    seg_part = lax.dynamic_slice_in_dim(gathered[2], block_offset, key_tile_block, 1).astype(
        jnp.float32
    )
    sequence_count = key_portion.shape[0]
    key_portion = key_portion.reshape(
        sequence_count, key_tile_block, KEY_VALUE_HEADS, HEAD_DIMENSION
    )
    value_portion = value_portion.reshape(
        sequence_count, key_tile_block, KEY_VALUE_HEADS, HEAD_DIMENSION
    )
    col_pos = block_offset + jnp.arange(key_tile_block, dtype=jnp.int32)
    return (key_portion, value_portion, seg_part, col_pos)


def masked_scores(query_block_list, key_portion, seg_rows, seg_part, row_pos, col_pos, score_scale):
    raw_scores = jnp.einsum(
        "skgtd,sjkd->skgtj", query_block_list, key_portion, preferred_element_type=jnp.float32
    )
    allowed = (seg_rows[:, :, None] == seg_part[:, None, :]) & (
        col_pos[None, None, :] <= row_pos[None, :, None]
    )
    allowed = allowed[:, None, None, :, :]
    return (jnp.where(allowed, raw_scores * score_scale, NEGATIVE), allowed)


def log_sum(
    query_block_list, gathered, seg_rows, row_pos, block_count, key_tile_block, score_scale
):
    lead_shape = query_block_list.shape[:4]

    def log_step_fn(block_index, carried):
        row_top, row_total = carried
        key_portion, value_portion, seg_part, col_pos = block_view(
            gathered, block_index, key_tile_block
        )
        scores, allowed = masked_scores(
            query_block_list, key_portion, seg_rows, seg_part, row_pos, col_pos, score_scale
        )
        new_top = jnp.maximum(row_top, jnp.max(scores, axis=-1))
        exponent = jnp.where(allowed, jnp.exp(scores - new_top[..., None]), 0.0)
        row_total = row_total * jnp.exp(row_top - new_top) + jnp.sum(exponent, axis=-1)
        return (new_top, row_total)

    start_state = (jnp.full(lead_shape, NEGATIVE, jnp.float32), jnp.zeros(lead_shape, jnp.float32))
    row_top, row_total = lax.fori_loop(0, block_count, log_step_fn, start_state)
    return row_top + jnp.log(row_total)


def attend(
    query_block_list,
    gathered,
    seg_rows,
    row_pos,
    block_count,
    key_tile_block,
    score_scale,
    log_total,
):

    def attend_step_fn(block_index, mixed_heads):
        key_portion, value_portion, seg_part, col_pos = block_view(
            gathered, block_index, key_tile_block
        )
        scores, allowed = masked_scores(
            query_block_list, key_portion, seg_rows, seg_part, row_pos, col_pos, score_scale
        )
        probabilities = jnp.where(allowed, jnp.exp(scores - log_total[..., None]), 0.0).astype(
            jnp.bfloat16
        )
        return mixed_heads + jnp.einsum(
            "skgtj,sjkd->skgtd", probabilities, value_portion, preferred_element_type=jnp.float32
        )

    return lax.fori_loop(
        0, block_count, attend_step_fn, jnp.zeros(query_block_list.shape, jnp.float32)
    )


def query_back(
    query_block_list,
    gathered,
    seg_rows,
    row_pos,
    block_count,
    key_tile_block,
    score_scale,
    log_total,
    gradient_reduced,
    row_delta,
):

    def query_step_fn(block_index, grad_query):
        key_portion, value_portion, seg_part, col_pos = block_view(
            gathered, block_index, key_tile_block
        )
        scores, allowed = masked_scores(
            query_block_list, key_portion, seg_rows, seg_part, row_pos, col_pos, score_scale
        )
        probabilities = jnp.where(allowed, jnp.exp(scores - log_total[..., None]), 0.0)
        grad_probs = jnp.einsum(
            "skgtd,sjkd->skgtj", gradient_reduced, value_portion, preferred_element_type=jnp.float32
        )
        grad_scores = (probabilities * (grad_probs - row_delta[..., None]) * score_scale).astype(
            jnp.bfloat16
        )
        return grad_query + jnp.einsum(
            "skgtj,sjkd->skgtd", grad_scores, key_portion, preferred_element_type=jnp.float32
        )

    return lax.fori_loop(
        0, block_count, query_step_fn, jnp.zeros(query_block_list.shape, jnp.float32)
    )


def key_back(
    key_local,
    value_local,
    seg_rows,
    row_pos,
    query_whole,
    grads_whole,
    stats_whole,
    seg_whole,
    first_block,
    block_count,
    query_tile,
    score_scale,
):
    sequence_count = key_local.shape[0]
    group_width = QUERY_HEADS // KEY_VALUE_HEADS

    def key_step_fn(block_index, carried):
        key_total, value_total = carried
        block_offset = block_index * query_tile
        query_rows = lax.dynamic_slice_in_dim(query_whole, block_offset, query_tile, 1).reshape(
            sequence_count, query_tile, KEY_VALUE_HEADS, group_width, HEAD_DIMENSION
        )
        grad_rows = lax.dynamic_slice_in_dim(grads_whole, block_offset, query_tile, 1).reshape(
            sequence_count, query_tile, KEY_VALUE_HEADS, group_width, HEAD_DIMENSION
        )
        log_rows = lax.dynamic_slice_in_dim(stats_whole[0], block_offset, query_tile, 3)
        delta_rows = lax.dynamic_slice_in_dim(stats_whole[1], block_offset, query_tile, 3)
        seg_query = lax.dynamic_slice_in_dim(seg_whole, block_offset, query_tile, 1).astype(
            jnp.float32
        )
        query_pos = block_offset + jnp.arange(query_tile, dtype=jnp.int32)
        raw_scores = jnp.einsum(
            "stkgd,sjkd->skgtj", query_rows, key_local, preferred_element_type=jnp.float32
        )
        allowed = (seg_query[:, :, None] == seg_rows[:, None, :]) & (
            row_pos[None, None, :] <= query_pos[None, :, None]
        )
        allowed = allowed[:, None, None, :, :]
        scores = jnp.where(allowed, raw_scores * score_scale, NEGATIVE)
        probabilities = jnp.where(allowed, jnp.exp(scores - log_rows[..., None]), 0.0)
        grad_probs = jnp.einsum(
            "stkgd,sjkd->skgtj", grad_rows, value_local, preferred_element_type=jnp.float32
        )
        grad_scores = (probabilities * (grad_probs - delta_rows[..., None]) * score_scale).astype(
            jnp.bfloat16
        )
        key_total = key_total + jnp.einsum(
            "skgtj,stkgd->sjkd", grad_scores, query_rows, preferred_element_type=jnp.float32
        )
        value_total = value_total + jnp.einsum(
            "skgtj,stkgd->sjkd",
            probabilities.astype(jnp.bfloat16),
            grad_rows,
            preferred_element_type=jnp.float32,
        )
        return (key_total, value_total)

    start_state = (jnp.zeros(key_local.shape, jnp.float32), jnp.zeros(key_local.shape, jnp.float32))
    return lax.fori_loop(first_block, block_count, key_step_fn, start_state)


def per_device(
    inputs,
    segments,
    weight_query,
    key_weight_matrix,
    value_weight_matrix,
    weight_out,
    weight_gate,
    weight_up,
    weight_down,
    gain_attention,
    gain_feed,
    cotangent,
):
    shards = (
        weight_query,
        key_weight_matrix,
        value_weight_matrix,
        weight_out,
        weight_gate,
        weight_up,
        weight_down,
    )
    gain_shards = (gain_attention, gain_feed)
    micro_count, sequence_count, token_count, model_width = inputs.shape
    group_width = QUERY_HEADS // KEY_VALUE_HEADS
    score_scale = 1.0 / math.sqrt(HEAD_DIMENSION)
    row_pos = lax.axis_index("seq") * token_count + jnp.arange(token_count, dtype=jnp.int32)
    cosine_table, sine_values = rope_tables(row_pos, HEAD_DIMENSION)
    key_span_length = token_count * lax.axis_size("seq")
    key_tile_block = min(512, key_span_length)
    total_blocks = key_span_length // key_tile_block
    block_count = row_pos[token_count - 1] // key_tile_block + 1
    first_block = row_pos[0] // key_tile_block
    outputs = []
    grad_list = []
    totals = jnp.zeros((4,), jnp.float32)
    gain_grads = jnp.zeros((2, model_width), jnp.float32)
    summed = None
    for batch_index in range(micro_count):
        weights_complete = gather_all(shards, gain_shards)
        tokens = inputs[batch_index].astype(jnp.float32)
        seg_local = segments[batch_index]
        seg_rows = seg_local.astype(jnp.float32)
        seg_low = seg_local.astype(jnp.bfloat16)
        gain_first = weights_complete[7].astype(jnp.float32)
        gain_second = weights_complete[8].astype(jnp.float32)
        norm_first, scale_first = norm_forward(tokens, gain_first)
        normalized = norm_first.astype(jnp.bfloat16)
        query_raw = apply_projection(normalized, weights_complete[0]).reshape(
            sequence_count, token_count, QUERY_HEADS, HEAD_DIMENSION
        )
        query_reduced = apply_rotation(query_raw, cosine_table, sine_values).astype(jnp.bfloat16)
        key_unrotated = apply_projection(normalized, weights_complete[1]).reshape(
            sequence_count, token_count, KEY_VALUE_HEADS, HEAD_DIMENSION
        )
        key_low = (
            apply_rotation(key_unrotated, cosine_table, sine_values)
            .astype(jnp.bfloat16)
            .reshape(sequence_count, token_count, KEY_VALUE_HEADS * HEAD_DIMENSION)
        )
        value_low = apply_projection(normalized, weights_complete[2]).astype(jnp.bfloat16)
        gathered = gather_keys(key_low, value_low, seg_low)
        query_block_list = query_reduced.reshape(
            sequence_count, token_count, KEY_VALUE_HEADS, group_width, HEAD_DIMENSION
        ).transpose(0, 2, 3, 1, 4)
        log_total = log_sum(
            query_block_list, gathered, seg_rows, row_pos, block_count, key_tile_block, score_scale
        )
        mixed_heads = attend(
            query_block_list,
            gathered,
            seg_rows,
            row_pos,
            block_count,
            key_tile_block,
            score_scale,
            log_total,
        )
        attn_low = (
            mixed_heads.transpose(0, 3, 1, 2, 4)
            .reshape(sequence_count, token_count, QUERY_HEADS * HEAD_DIMENSION)
            .astype(jnp.bfloat16)
        )
        branch_attn = apply_projection(attn_low, weights_complete[3])
        hidden = tokens + branch_attn
        norm_second, scale_second = norm_forward(hidden, gain_second)
        normed_second = norm_second.astype(jnp.bfloat16)
        gate_values = apply_projection(normed_second, weights_complete[4])
        up_values = apply_projection(normed_second, weights_complete[5])
        gate_sigmoid = jax.nn.sigmoid(gate_values)
        inner_low = (gate_values * gate_sigmoid * up_values).astype(jnp.bfloat16)
        branch_feed = apply_projection(inner_low, weights_complete[6])
        result = hidden + branch_feed
        outputs.append(result.astype(jnp.bfloat16))
        valid_rows = (seg_local != 0).astype(jnp.float32)[:, :, None]
        totals = totals + jnp.stack(
            [
                jnp.sum(valid_rows * branch_attn * branch_attn),
                jnp.sum(valid_rows * branch_feed * branch_feed),
                jnp.sum(valid_rows * result * result),
                jnp.sum(valid_rows),
            ]
        )
        back_weights = gather_all(shards, gain_shards)
        back_keys = gather_keys(key_low, value_low, seg_low)
        grad_result = cotangent[batch_index].astype(jnp.float32)
        grad_feed = grad_result.astype(jnp.bfloat16)
        grad_down = weight_grad(inner_low, grad_feed)
        grad_inner = project_back(grad_feed, back_weights[6])
        grad_up = (grad_inner * gate_values * gate_sigmoid).astype(jnp.bfloat16)
        grad_gate = (
            grad_inner * up_values * gate_sigmoid * (1.0 + gate_values * (1.0 - gate_sigmoid))
        ).astype(jnp.bfloat16)
        grad_gate_w = weight_grad(normed_second, grad_gate)
        grad_up_w = weight_grad(normed_second, grad_up)
        grad_normed_second = project_back(grad_gate, back_weights[4]) + project_back(
            grad_up, back_weights[5]
        )
        grad_hidden_norm, grad_gain_second = norm_backward(
            hidden, scale_second, gain_second, grad_normed_second
        )
        grad_hidden = grad_result + grad_hidden_norm
        grad_branch = grad_hidden.astype(jnp.bfloat16)
        grad_out_w = weight_grad(attn_low, grad_branch)
        mixed_gradient = project_back(grad_branch, back_weights[3]).astype(jnp.bfloat16)
        gradient_reduced = mixed_gradient.reshape(
            sequence_count, token_count, KEY_VALUE_HEADS, group_width, HEAD_DIMENSION
        ).transpose(0, 2, 3, 1, 4)
        row_delta = jnp.sum(gradient_reduced.astype(jnp.float32) * mixed_heads, axis=-1)
        grad_query = query_back(
            query_block_list,
            back_keys,
            seg_rows,
            row_pos,
            block_count,
            key_tile_block,
            score_scale,
            log_total,
            gradient_reduced,
            row_delta,
        )
        query_flat = query_reduced.reshape(
            sequence_count, token_count, QUERY_HEADS * HEAD_DIMENSION
        )
        query_whole, grads_whole = (
            lax.all_gather(query_flat, "seq", axis=1, tiled=True),
            lax.all_gather(mixed_gradient, "seq", axis=1, tiled=True),
        )
        stats_whole = (
            lax.all_gather(log_total, "seq", axis=3, tiled=True),
            lax.all_gather(row_delta, "seq", axis=3, tiled=True),
        )
        key_local = key_low.reshape(sequence_count, token_count, KEY_VALUE_HEADS, HEAD_DIMENSION)
        value_local = value_low.reshape(
            sequence_count, token_count, KEY_VALUE_HEADS, HEAD_DIMENSION
        )
        key_total, value_total = key_back(
            key_local,
            value_local,
            seg_rows,
            row_pos,
            query_whole,
            grads_whole,
            stats_whole,
            back_keys[2],
            first_block,
            total_blocks,
            key_tile_block,
            score_scale,
        )
        key_grad_low = (
            reverse_rotation(key_total, cosine_table, sine_values)
            .reshape(sequence_count, token_count, KEY_VALUE_HEADS * HEAD_DIMENSION)
            .astype(jnp.bfloat16)
        )
        value_grad_low = value_total.reshape(
            sequence_count, token_count, KEY_VALUE_HEADS * HEAD_DIMENSION
        ).astype(jnp.bfloat16)
        query_grad = grad_query.transpose(0, 3, 1, 2, 4).reshape(
            sequence_count, token_count, QUERY_HEADS, HEAD_DIMENSION
        )
        query_grad_low = (
            reverse_rotation(query_grad, cosine_table, sine_values)
            .reshape(sequence_count, token_count, QUERY_HEADS * HEAD_DIMENSION)
            .astype(jnp.bfloat16)
        )
        grad_normed = (
            project_back(query_grad_low, back_weights[0])
            + project_back(key_grad_low, back_weights[1])
            + project_back(value_grad_low, back_weights[2])
        )
        grad_token_norm, grad_gain_first = norm_backward(
            tokens, scale_first, gain_first, grad_normed
        )
        grad_list.append((grad_hidden + grad_token_norm).astype(jnp.bfloat16))
        gain_grads = gain_grads + jnp.stack([grad_gain_first, grad_gain_second])
        batch_grads = (
            weight_grad(normalized, query_grad_low),
            weight_grad(normalized, key_grad_low),
            weight_grad(normalized, value_grad_low),
            grad_out_w,
            grad_gate_w,
            grad_up_w,
            grad_down,
        )
        summed = batch_grads if summed is None else jax.tree.map(jnp.add, summed, batch_grads)
    reduced = reduce_grads(summed)
    gain_total, totals = lax.psum((gain_grads, totals), ("dp", "seq"))
    piece_width = model_width // lax.axis_size("seq")
    gain_part = lax.dynamic_slice_in_dim(
        gain_total, lax.axis_index("seq") * piece_width, piece_width, 1
    )
    root_means = jnp.sqrt(totals[:3] / (totals[3] * model_width))
    return (
        jnp.stack(outputs),
        jnp.stack(grad_list),
        reduced[0],
        reduced[1],
        reduced[2],
        reduced[3],
        reduced[4],
        reduced[5],
        reduced[6],
        gain_part[0],
        gain_part[1],
        root_means,
    )


def solution(mesh):
    placed = (
        P(None, "dp", "seq", None),
        P(None, "dp", "seq"),
        P("seq", "dp"),
        P("seq", "dp"),
        P("seq", "dp"),
        P("seq", "dp"),
        P("seq", "dp"),
        P("seq", "dp"),
        P("seq", "dp"),
        P("seq"),
        P("seq"),
        P(None, "dp", "seq", None),
    )
    return jax.shard_map(
        per_device,
        mesh=mesh,
        in_specs=placed,
        out_specs=(
            P(None, "dp", "seq", None),
            P(None, "dp", "seq", None),
            P("seq", "dp"),
            P("seq", "dp"),
            P("seq", "dp"),
            P("seq", "dp"),
            P("seq", "dp"),
            P("seq", "dp"),
            P("seq", "dp"),
            P("seq"),
            P("seq"),
            P(),
        ),
        check_vma=False,
    )
```

profile of v0, /device:TPU:0, one launch (start us, length us, event | category | flops | bytes accessed | tf_op | source)
XLA Modules:
  0.0 2115.3 jit_solution(4461957145483871647)
XLA Ops:
  7.3 6.7 all-gather.13
  15.0 5.4 all-gather.15
  21.5 6.7 all_gather.75
  28.3 7.5 all_gather.73
  35.9 7.3 all-gather.16
  51.1 58.4 %all-reduce.13 = (bf16[1024]{0:T(1024)(128)(2,1)S(1)}, bf16[1152]{0:T(1024)(128)(2,1)S(1)}, bf16[1152]{0:T(1024)(128)(2,1)S(1)}, bf16[1024]{0:T(1024)(128)(2,1)S(1)}) all-reduce(bf16[1024]{0:T(1024)(128)(2,1)S(1)} %dynamic-update-slice.3, bf16[1152]{0:T(1024)(128)(2,1)S(1)} %dynamic-update-slice.1, ...), channel_id=5, replica_groups=mesh['dp'=2,'seq'=16] {'seq'}, use_global_device_ids=true, to_apply=%add.3 | all-reduce | flops 4352 | bytes 17408
  109.5 4.6 all-gather.12
  114.3 4.6 all-gather.14
  119.1 22.3 %all_gather.68 = bf16[1152,384]{1,0:T(8,128)(2,1)S(1)} all-gather(bf16[72,384]{1,0:T(8,128)(2,1)S(1)} %bitcast.949), channel_id=1, replica_groups=mesh['dp'=2,'seq'=16] {'seq'}, dimensions={0}, use_global_device_ids=true | all-gather | bytes 940032 | tf_op jit(solution)/shard_map/all_gather | solution.py:77
  142.7 25.5 %all_gather.63 = bf16[1152,384]{1,0:T(8,128)(2,1)S(1)} all-gather(bf16[72,384]{1,0:T(8,128)(2,1)S(1)} %bitcast.948), channel_id=1, replica_groups=mesh['dp'=2,'seq'=16] {'seq'}, dimensions={0}, use_global_device_ids=true | all-gather | bytes 940032 | tf_op jit(solution)/shard_map/all_gather | solution.py:76
  173.2 22.6 %all-gather.5 = bf16[1024,384]{1,0:T(8,128)(2,1)S(1)} all-gather(bf16[64,384]{1,0:T(8,128)(2,1)S(1)} %convolution_convert_fusion.2), channel_id=7, replica_groups=mesh['dp'=2,'seq'=16] {'seq'}, dimensions={0}, use_global_device_ids=true | all-gather | bytes 835584 | tf_op jit(solution)/shard_map/all_gather | solution.py:90
  197.0 23.0 %all-gather.2 = bf16[1024,384]{1,0:T(8,128)(2,1)S(1)} all-gather(bf16[64,384]{1,0:T(8,128)(2,1)S(1)} %convolution_convert_fusion.3), channel_id=4, replica_groups=mesh['dp'=2,'seq'=16] {'seq'}, dimensions={0}, use_global_device_ids=true | all-gather | bytes 835584 | tf_op jit(solution)/shard_map/all_gather | solution.py:90
  222.8 25.1 %all-gather.1 = bf16[1024,384]{1,0:T(8,128)(2,1)S(1)} all-gather(bf16[64,384]{1,0:T(8,128)(2,1)S(1)} %get-tuple-element.1299), channel_id=3, replica_groups=mesh['dp'=2,'seq'=16] {'seq'}, dimensions={0}, use_global_device_ids=true | all-gather | bytes 835584 | tf_op jit(solution)/shard_map/all_gather | solution.py:89
  248.2 23.0 %all-gather.4 = bf16[1024,384]{1,0:T(8,128)(2,1)S(1)} all-gather(bf16[64,384]{1,0:T(8,128)(2,1)S(1)} %get-tuple-element.1300), channel_id=6, replica_groups=mesh['dp'=2,'seq'=16] {'seq'}, dimensions={0}, use_global_device_ids=true | all-gather | bytes 835584 | tf_op jit(solution)/shard_map/all_gather | solution.py:89
  293.8 3.9 fusion.166
  301.4 4.1 while.97
  315.9 3.5 while.98
  330.9 5.4 fusion.256
  336.2 5.3 fusion.255
  341.5 5.8 multiply_convert_fusion.2
  349.7 5.5 convolution_add_fusion.12
  380.1 38.0 %all_gather.167 = f32[1,6,3,1024]{1,0,2,3:T(1,128)S(1)} all-gather(f32[1,6,3,64]{1,0,2,3:T(1,128)} %copy-done.73), channel_id=1, replica_groups=mesh['dp'=2,'seq'=16] {'seq'}, dimensions={3}, use_global_device_ids=true | all-gather | bytes 78336 | tf_op jit(solution)/shard_map/all_gather | solution.py:466
  421.2 26.9 %all_gather.163 = f32[1,6,3,1024]{1,0,2,3:T(1,128)S(1)} all-gather(f32[1,6,3,64]{1,0,2,3:T(1,128)S(1)} %add.443), channel_id=1, replica_groups=mesh['dp'=2,'seq'=16] {'seq'}, dimensions={3}, use_global_device_ids=true | all-gather | bytes 78336 | tf_op jit(solution)/shard_map/all_gather | solution.py:466
  459.4 7.1 fusion.210
  466.5 7.0 fusion.263
  473.5 7.0 fusion.262
  484.9 7.4 while.102
  498.7 7.3 while.100
  512.4 45.7 %all-gather.8 = f32[6,3,1024]{0,1,2:T(4,128)S(1)} all-gather(f32[6,3,64]{0,1,2:T(4,128)} %copy.206), channel_id=10, replica_groups=mesh['dp'=2,'seq'=16] {'seq'}, dimensions={2}, use_global_device_ids=true | all-gather | bytes 78336 | tf_op jit(solution)/shard_map/all_gather | solution.py:467
  559.5 30.0 %all-gather.11 = f32[6,3,1024]{0,1,2:T(4,128)S(1)} all-gather(f32[6,3,64]{0,1,2:T(4,128)} %copy.224), channel_id=13, replica_groups=mesh['dp'=2,'seq'=16] {'seq'}, dimensions={2}, use_global_device_ids=true | all-gather | bytes 78336 | tf_op jit(solution)/shard_map/all_gather | solution.py:467
  591.3 5.7 convolution_add_fusion.3
  597.1 4.5 reshape.2364
  605.8 4.5 reshape.2361
  610.4 12.1 convolution_add_fusion
  622.5 14.4 reshape.2367
  636.9 12.0 convolution_add_fusion.1
  648.9 14.3 reshape.2366
  663.2 12.0 convolution_add_fusion.2
  675.2 14.5 reshape.2365
  692.8 27.3 %while.101 = (s32[]{:T(128)}, f32[1,64,6,64]{1,3,2,0:T(8,128)}, f32[1,64,6,64]{1,3,2,0:T(8,128)}, bf16[1,1024,1152]{2,1,0:T(8,128)(2,1)}, bf16[1,1024]{1,0:T(2,1...) while((s32[]{:T(128)}, f32[1,64,6,64]{1,3,2,0:T(8,128)}, ...), condition=%wide.region_21.22_spmd.clone, body=%wide.region_20.21_spmd.clone.sunk | while | flops 307446848 | bytes 22022104 | solution.py:313
  726.9 26.0 %while.103 = (s32[]{:T(128)}, f32[1,64,6,64]{1,3,2,0:T(8,128)}, f32[1,64,6,64]{1,3,2,0:T(8,128)}, bf16[1,1024,1152]{2,1,0:T(8,128)(2,1)}, bf16[1,1024]{1,0:T(2,1...) while((s32[]{:T(128)}, f32[1,64,6,64]{1,3,2,0:T(8,128)}, ...), condition=%wide.region_28.29_spmd.clone, body=%wide.region_27.28_spmd.clone.sunk | while | flops 307446848 | bytes 22022104 | solution.py:313
  766.4 1202.8 %all-reduce.15 = (bf16[16,82944]{1,0:T(8,128)(2,1)}, bf16[16,27648]{1,0:T(8,128)(2,1)}, bf16[16,27648]{1,0:T(8,128)(2,1)}, bf16[16,82944]{1,0:T(8,128)(2,1)}, bf...) all-reduce(f32[16,82944]{1,0:T(8,128)} %reshape.2361, ...), channel_id=14, replica_groups=mesh['dp'=2,'seq'=16] {'seq'}, use_global_device_ids=true, to_apply=%region_30.31.clone | all-reduce | flops 14155776 | bytes 84934656
  1984.7 5.7 maximum_add_fusion.1
  1990.4 3.6 fusion.168
  2004.6 10.7 fusion.142
  2019.9 10.4 fusion.144
  2031.4 47.0 %all-reduce.11 = (f32[2,1152]{1,0:T(2,128)S(1)}, f32[4]{0:T(128)S(1)}) all-reduce(f32[2,1152]{1,0:T(2,128)S(1)} %maximum_add_fusion, f32[4]{0:T(128)S(1)} %copy-done.112), channel_id=1, replica_groups=mesh['dp'=2,'seq'=16] {'dp','seq'}, use_global_device_ids=true, to_apply=%region_48.49 | all-reduce | flops 2308 | bytes 18464 | tf_op jit(solution)/shard_map/psum | solution.py:524
  2079.0 10.4 fusion.143
  (608 shorter events, 281.5 us)
Async XLA Ops:
  7.2 21.1 copy-start.93
  7.2 28.7 %copy-start.88 = (bf16[192,576]{1,0:T(8,128)(2,1)S(1)}, bf16[192,576]{1,0:T(8,128)(2,1)}, u32[]{:S(2)}) copy-start(bf16[192,576]{1,0:T(8,128)(2,1)} %param.36) | copy-start | bytes 663556
  7.2 265.2 %all-gather.27.cloned.1.call-start = ((), (), s32[]{:S(2)}) async-start(), calls=%async_computation.7 | async-start | bytes 2820096 | tf_op jit(solution)/shard_map/all_gather | solution.py:75
  14.9 309.6 %all-gather.29.cloned.1.call-start = ((), (), s32[]{:S(2)}) async-start(), calls=%async_computation.8 | async-start | bytes 2820096 | tf_op jit(solution)/shard_map/all_gather | solution.py:78
  21.4 309.5 %all-gather.33.cloned.1.call-start = ((), (), s32[]{:S(2)}) async-start(), calls=%async_computation.10 | async-start | bytes 7520256 | tf_op jit(solution)/shard_map/all_gather | solution.py:80
  28.2 19.3 copy-start.107
  28.2 19.9 copy-start.111
  28.2 21.8 %copy-start.6 = (bf16[2,1,64,1152]{3,2,1,0:T(8,128)(2,1)S(1)}, bf16[2,1,64,1152]{3,2,1,0:T(8,128)(2,1)}, u32[]{:S(2)}) copy-start(bf16[2,1,64,1152]{3,2,1,0:T(8,128)(2,1)} %param.28) | copy-start | bytes 884740
  28.2 22.4 %copy-start.115 = (bf16[72]{0:T(256)(128)(2,1)S(1)}, bf16[72]{0:T(256)(128)(2,1)}, u32[]{:S(2)}) copy-start(bf16[72]{0:T(256)(128)(2,1)} %param.37) | copy-start | bytes 436
  28.2 22.6 %copy-start.116 = (bf16[72]{0:T(256)(128)(2,1)S(1)}, bf16[72]{0:T(256)(128)(2,1)}, u32[]{:S(2)}) copy-start(bf16[72]{0:T(256)(128)(2,1)} %param.38) | copy-start | bytes 436
  28.2 81.2 %copy-start.101 = (bf16[72,192]{1,0:T(8,128)(2,1)S(1)}, bf16[72,192]{1,0:T(8,128)(2,1)}, u32[]{:S(2)}) copy-start(bf16[72,192]{1,0:T(8,128)(2,1)} %param.31) | copy-start | bytes 82948
  28.2 86.0 %copy-start.102 = (bf16[72,192]{1,0:T(8,128)(2,1)S(1)}, bf16[72,192]{1,0:T(8,128)(2,1)}, u32[]{:S(2)}) copy-start(bf16[72,192]{1,0:T(8,128)(2,1)} %param.32) | copy-start | bytes 82948
  28.3 308.0 %all-gather.31.cloned.1.call-start = ((), (), s32[]{:S(2)}) async-start(), calls=%async_computation.9 | async-start | bytes 7520256 | tf_op jit(solution)/shard_map/all_gather | solution.py:79
  35.8 305.7 %all-gather.35.cloned.1.call-start = ((), (), s32[]{:S(2)}) async-start(), calls=%async_computation.11 | async-start | bytes 7520256 | tf_op jit(solution)/shard_map/all_gather | solution.py:81
  44.9 646.5 %all-gather.37.cloned.1.call-start = ((), (), s32[]{:S(2)}) async-start(), calls=%async_computation.14 | async-start | bytes 2506752 | tf_op jit(solution)/shard_map/all_gather | solution.py:462
  109.5 166.9 %copy-start.40 = (f32[1152]{0:T(1024)}, f32[1152]{0:T(1024)S(1)}, u32[]{:S(2)}) copy-start(f32[1152]{0:T(1024)S(1)} %convert_element_type.629) | copy-start | bytes 13828
  142.0 130.4 %copy-start.95 = (f32[64]{0:T(128)}, f32[64]{0:T(128)S(1)}, u32[]{:S(2)}) copy-start(f32[64]{0:T(128)S(1)} %get-tuple-element.1340) | copy-start | bytes 772
  142.0 134.3 %copy-start.98 = (f32[64]{0:T(128)}, f32[64]{0:T(128)S(1)}, u32[]{:S(2)}) copy-start(f32[64]{0:T(128)S(1)} %get-tuple-element.1329) | copy-start | bytes 772
  142.3 30.9 %copy-start.82 = (bf16[64,384]{1,0:T(8,128)(2,1)}, bf16[64,384]{1,0:T(8,128)(2,1)S(1)}, u32[]{:S(2)}) copy-start(bf16[64,384]{1,0:T(8,128)(2,1)S(1)} %convolution_convert_fusion.2) | copy-start | bytes 147460
  142.7 54.3 %copy-start.84 = (bf16[64,384]{1,0:T(8,128)(2,1)}, bf16[64,384]{1,0:T(8,128)(2,1)S(1)}, u32[]{:S(2)}) copy-start(bf16[64,384]{1,0:T(8,128)(2,1)S(1)} %convolution_convert_fusion.3) | copy-start | bytes 147460
  171.1 122.7 %copy-start.42 = (f32[64,64]{1,0:T(8,128)}, f32[64,64]{1,0:T(8,128)S(1)}, u32[]{:S(2)}) copy-start(f32[64,64]{1,0:T(8,128)S(1)} %get-tuple-element.1313) | copy-start | bytes 49156
  171.1 122.7 %copy-start.45 = (f32[64,64]{1,0:T(8,128)}, f32[64,64]{1,0:T(8,128)S(1)}, u32[]{:S(2)}) copy-start(f32[64,64]{1,0:T(8,128)S(1)} %get-tuple-element.1314) | copy-start | bytes 49156
  330.2 361.2 %all-gather.39.cloned.1.call-start = ((), (), s32[]{:S(2)}) async-start(), calls=%async_computation.15 | async-start | bytes 2506752 | tf_op jit(solution)/shard_map/all_gather | solution.py:463
  371.6 84.5 %copy-start.21 = (f32[64,1152]{1,0:T(8,128)}, f32[64,1152]{1,0:T(8,128)S(1)}, u32[]{:S(2)}) copy-start(f32[64,1152]{1,0:T(8,128)S(1)} %get-tuple-element.1287) | copy-start | bytes 884740
  373.2 352.3 %all-gather.41.cloned.1.call-start = ((), (), s32[]{:S(2)}) async-start(), calls=%async_computation.16 | async-start | bytes 2506752 | tf_op jit(solution)/shard_map/all_gather | solution.py:462
  374.0 351.6 %all-gather.43.cloned.1.call-start = ((), (), s32[]{:S(2)}) async-start(), calls=%async_computation.17 | async-start | bytes 2506752 | tf_op jit(solution)/shard_map/all_gather | solution.py:463
  480.5 1612.7 %reduce-scatter.24.cloned.1.call-start = ((), (), s32[]{:S(2)}) async-start(), calls=%async_computation.19 | async-start | bytes 147456
  559.5 31.8 %copy-start.23 = (f32[64,1152]{1,0:T(8,128)S(1)}, f32[64,1152]{1,0:T(8,128)}, u32[]{:S(2)}) copy-start(f32[64,1152]{1,0:T(8,128)} %get-tuple-element.1288) | copy-start | bytes 884740
  559.5 31.8 %copy-start.61 = (bf16[64,1152]{1,0:T(8,128)(2,1)S(1)}, bf16[64,1152]{1,0:T(8,128)(2,1)}, u32[]{:S(2)}) copy-start(bf16[64,1152]{1,0:T(8,128)(2,1)} %copy-done.60) | copy-start | bytes 442372
  766.3 1205.7 %copy-start.76 = (bf16[1,1,64,1152]{3,2,1,0:T(8,128)(2,1)S(1)}, bf16[1,1,64,1152]{3,2,1,0:T(8,128)(2,1)}, u32[]{:S(2)}) copy-start(bf16[1,1,64,1152]{3,2,1,0:T(8,128)(2,1)} %get-tuple-element.1283) | copy-start | bytes 442372
  766.3 1205.7 %copy-start.77 = (bf16[1,1,64,1152]{3,2,1,0:T(8,128)(2,1)S(1)}, bf16[1,1,64,1152]{3,2,1,0:T(8,128)(2,1)}, u32[]{:S(2)}) copy-start(bf16[1,1,64,1152]{3,2,1,0:T(8,128)(2,1)} %get-tuple-element.1284) | copy-start | bytes 442372
  766.3 1206.5 %copy-start.103 = (f32[1152]{0:T(1024)S(1)}, f32[1152]{0:T(1024)}, u32[]{:S(2)}) copy-start(f32[1152]{0:T(1024)} %get-tuple-element.1041) | copy-start | bytes 13828
  766.4 1207.1 %copy-start.104 = (f32[1152]{0:T(1024)S(1)}, f32[1152]{0:T(1024)}, u32[]{:S(2)}) copy-start(f32[1152]{0:T(1024)} %get-tuple-element.1043) | copy-start | bytes 13828
  766.4 1207.7 %copy-start.15 = (f32[1,6,3,64,64]{4,3,2,1,0:T(8,128)S(1)}, f32[1,6,3,64,64]{4,3,2,1,0:T(8,128)}, u32[]{:S(2)}) copy-start(f32[1,6,3,64,64]{4,3,2,1,0:T(8,128)} %get-tuple-element.477) | copy-start | bytes 884740
  1972.0 122.7 %reduce-scatter.26.cloned.1.call-start = ((), (), s32[]{:S(2)}) async-start(), calls=%async_computation.20 | async-start | bytes 147456
  1975.3 22.4 %copy-start.2 = (bf16[1152,1152]{1,0:T(8,128)(2,1)S(1)}, bf16[1152,1152]{1,0:T(8,128)(2,1)}, u32[]{:S(2)}) copy-start(bf16[1152,1152]{1,0:T(8,128)(2,1)} %all-gather.27.cloned.1.call-done) | copy-start | bytes 7962628
  1975.3 22.4 %copy-start.29 = (f32[64,1152]{1,0:T(8,128)S(1)}, f32[64,1152]{1,0:T(8,128)}, u32[]{:S(2)}) copy-start(f32[64,1152]{1,0:T(8,128)} %mul.988) | copy-start | bytes 884740
  1984.6 111.6 %reduce-scatter.22.cloned.1.call-start = ((), (), s32[]{:S(2)}) async-start(), calls=%async_computation.18 | async-start | bytes 442368
  1997.6 100.3 %reduce-scatter.28.cloned.1.call-start = ((), (), s32[]{:S(2)}) async-start(), calls=%async_computation.21 | async-start | bytes 442368
  2000.3 16.6 copy-start.65
  2000.3 16.6 copy-start.87
  2004.6 95.2 %reduce-scatter.30.cloned.1.call-start = ((), (), s32[]{:S(2)}) async-start(), calls=%async_computation.22 | async-start | bytes 884736
  2017.4 84.3 %reduce-scatter.18.cloned.1.call-start = ((), (), s32[]{:S(2)}) async-start(), calls=%async_computation.12 | async-start | bytes 663552 | tf_op jit(solution)/shard_map/reduce_scatter | solution.py:124
  2030.2 61.9 %copy-start.22 = (f32[64,1152]{1,0:T(8,128)S(1)}, f32[64,1152]{1,0:T(8,128)}, u32[]{:S(2)}) copy-start(f32[64,1152]{1,0:T(8,128)} %copy-done.21) | copy-start | bytes 884740
  2030.3 61.9 %copy-start.24 = (f32[64,1152]{1,0:T(8,128)S(1)}, f32[64,1152]{1,0:T(8,128)}, u32[]{:S(2)}) copy-start(f32[64,1152]{1,0:T(8,128)} %get-tuple-element.1288) | copy-start | bytes 884740
  2030.3 61.9 %copy-start.113 = (f32[64]{0:T(128)S(1)}, f32[64]{0:T(128)}, u32[]{:S(2)}) copy-start(f32[64]{0:T(128)} %get-tuple-element.1328) | copy-start | bytes 772
  2030.3 61.9 %copy-start.114 = (f32[64]{0:T(128)S(1)}, f32[64]{0:T(128)}, u32[]{:S(2)}) copy-start(f32[64]{0:T(128)} %get-tuple-element.1341) | copy-start | bytes 772
  2031.3 75.3 %reduce-scatter.20.cloned.1.call-start = ((), (), s32[]{:S(2)}) async-start(), calls=%async_computation.13 | async-start | bytes 663552 | tf_op jit(solution)/shard_map/reduce_scatter | solution.py:127
  (89 other events, 456.8 us)
Sparse Core Ops, SparseCore 0:
  15.0 44.8 all-gather.26
  62.6 42.1 all-gather.28
  107.2 77.5 all-gather.32
  186.9 78.2 all-gather.30
  268.0 65.1 all-gather.34
  335.3 47.1 all-gather.36
  384.9 45.1 all-gather.38
  432.4 44.0 all-gather.40
  480.6 46.0 all-gather.42
  1972.1 16.6 reduce-scatter.23
  1991.1 10.3 reduce-scatter.25
  2004.1 12.3 reduce-scatter.21
  2018.8 12.0 reduce-scatter.27
  2033.0 15.6 reduce-scatter.29
  2051.4 13.8 reduce-scatter.17
  2091.7 14.7 reduce-scatter.19
where the time goes:
time: 2130 us; the launch traced here: 2120 us
  blocking collectives  1630 us (77%)
  local copies, waits for them, and re-layouts  221 us (10%)
  matrix products  184 us (9%)
  other arithmetic  48.2 us (2%)
  between operations  23.2 us (1%)
    unnamed x2, blocking collectives  1260 us
    dot_general x14, matrix products, weight_grad(): jnp.einsum('std,stf->df', acts_low, grads_low, preferred_element_type=jnp...  78.7 us
    all_gather x2, blocking collectives, per_device(): lax.all_gather(row_delta, 'seq', axis=3, tiled=True)  75.7 us
    all_gather x2, blocking collectives, per_device(): lax.all_gather(log_total, 'seq', axis=3, tiled=True)  64.9 us
    reshape x7, local copies, waits for them, and re-layouts, reduce_grads(): flat = [grad_item.reshape(seq_count, -1) for grad_item in grads]  57 us
    all_gather x2, blocking collectives, gather_keys(): lax.all_gather(key_low, 'seq', axis=1, tiled=True)  48.1 us
    psum x1, blocking collectives, per_device(): gain_total, totals = lax.psum((gain_grads, totals), ('dp', 'seq'))  47 us
    all_gather x2, blocking collectives, gather_keys(): lax.all_gather(value_low, 'seq', axis=1, tiled=True)  45.6 us
  transfers between devices with their start and end apart: 16, of which 1 were waited for; matrix products, arithmetic and copies ran while one was open for 19% of the time, Pallas kernels for 0%

commit v1 on v0

--- a/solution.py
+++ b/solution.py
@@ -93,43 +93,13 @@
 
 
 def reduce_grads(grads):
-    seq_count = lax.axis_size("seq")
-    flat = [grad_item.reshape(seq_count, -1) for grad_item in grads]
-    row_parts = (
-        lax.psum_scatter(flat[0], "seq", scatter_dimension=0, tiled=True),
-        lax.psum_scatter(flat[1], "seq", scatter_dimension=0, tiled=True),
-        lax.psum_scatter(flat[2], "seq", scatter_dimension=0, tiled=True),
-        lax.psum_scatter(flat[3], "seq", scatter_dimension=0, tiled=True),
-        lax.psum_scatter(flat[4], "seq", scatter_dimension=0, tiled=True),
-        lax.psum_scatter(flat[5], "seq", scatter_dimension=0, tiled=True),
-        lax.psum_scatter(flat[6], "seq", scatter_dimension=0, tiled=True),
-    )
-    pieces = [
-        part_item.reshape(grad_item.shape[0] // seq_count, grad_item.shape[1])
-        for part_item, grad_item in zip(row_parts, grads)
+    rows = [
+        lax.psum_scatter(g.astype(jnp.bfloat16), "seq", scatter_dimension=0, tiled=True)
+        for g in grads
     ]
-    return (
-        lax.psum_scatter(
-            pieces[0].astype(jnp.bfloat16), "dp", scatter_dimension=1, tiled=True
-        ).astype(jnp.float32),
-        lax.psum_scatter(
-            pieces[1].astype(jnp.bfloat16), "dp", scatter_dimension=1, tiled=True
-        ).astype(jnp.float32),
-        lax.psum_scatter(
-            pieces[2].astype(jnp.bfloat16), "dp", scatter_dimension=1, tiled=True
-        ).astype(jnp.float32),
-        lax.psum_scatter(
-            pieces[3].astype(jnp.bfloat16), "dp", scatter_dimension=1, tiled=True
-        ).astype(jnp.float32),
-        lax.psum_scatter(
-            pieces[4].astype(jnp.bfloat16), "dp", scatter_dimension=1, tiled=True
-        ).astype(jnp.float32),
-        lax.psum_scatter(
-            pieces[5].astype(jnp.bfloat16), "dp", scatter_dimension=1, tiled=True
-        ).astype(jnp.float32),
-        lax.psum_scatter(
-            pieces[6].astype(jnp.bfloat16), "dp", scatter_dimension=1, tiled=True
-        ).astype(jnp.float32),
+    return tuple(
+        lax.psum_scatter(r, "dp", scatter_dimension=1, tiled=True).astype(jnp.float32)
+        for r in rows
     )
 
 
@@ -352,8 +322,8 @@
     totals = jnp.zeros((4,), jnp.float32)
     gain_grads = jnp.zeros((2, model_width), jnp.float32)
     summed = None
+    weights_complete = gather_all(shards, gain_shards)
     for batch_index in range(micro_count):
-        weights_complete = gather_all(shards, gain_shards)
         tokens = inputs[batch_index].astype(jnp.float32)
         seg_local = segments[batch_index]
         seg_rows = seg_local.astype(jnp.float32)
@@ -417,8 +387,8 @@
                 jnp.sum(valid_rows),
             ]
         )
-        back_weights = gather_all(shards, gain_shards)
-        back_keys = gather_keys(key_low, value_low, seg_low)
+        back_weights = weights_complete
+        back_keys = gathered
         grad_result = cotangent[batch_index].astype(jnp.float32)
         grad_feed = grad_result.astype(jnp.bfloat16)
         grad_down = weight_grad(inner_low, grad_feed)

time: 2130 us -> 1200 us (0.56)
  blocking collectives: 1630 us -> 445 us
  waiting for transfers between devices: 4.17 us -> 403 us
  local copies, waits for them, and re-layouts: 221 us -> 124 us
  matrix products: 184 us -> 145 us
    unnamed x2 -> x1, blocking collectives: 1260 us -> 58.8 us
    reduce_scatter x2 -> x5, waiting for transfers between devices: 3.16 us -> 262 us  [the longest x3 233 us: reduce_grads(): lax.psum_scatter(g.astype(jnp.bfloat16), 'seq', scatter_dimension=0, tile...]
    unnamed x21 -> x32, waiting for transfers between devices: 0.95 us -> 141 us
    reshape x7 -> x0, local copies, waits for them, and re-layouts: 57 us -> none  [reduce_grads(): flat = [grad_item.reshape(seq_count, -1) for grad_item in grads]]
    convert_element_type x14 -> x0, local copies, waits for them, and re-layouts: 48.7 us -> none  [the longest x2 11.3 us: reduce_grads(): pieces[4].astype(jnp.bfloat16)]
    dot_general x14, matrix products: 78.7 us -> 41.4 us  [weight_grad(): jnp.einsum('std,stf->df', acts_low, grads_low, preferred_element_type=jnp...]
    all_gather x2, blocking collectives: 64.9 us -> 86.4 us  [per_device(): lax.all_gather(log_total, 'seq', axis=3, tiled=True)]
    unnamed x286 -> x282, local copies, waits for them, and re-layouts: 40.8 us -> 44.9 us
  transfers between devices with their start and end apart: 16 -> 23, of which waited for: 1 -> 13; matrix products, arithmetic and copies ran while one was open for 19% -> 26% of each run, Pallas kernels for 0% -> 0%
where the time goes in v1:
time: 1200 us; the launch traced here: 1190 us
  blocking collectives  445 us (37%)
  waiting for transfers between devices  403 us (34%)
  matrix products  145 us (12%)
  local copies, waits for them, and re-layouts  124 us (10%)
  other arithmetic  50.4 us (4%)
  between operations  23 us (2%)
    reduce_scatter x3, waiting for transfers between devices, reduce_grads(): lax.psum_scatter(g.astype(jnp.bfloat16), 'seq', scatter_dimension=0, tile...  233 us
    unnamed x32, waiting for transfers between devices  141 us
    all_gather x2, blocking collectives, per_device(): lax.all_gather(log_total, 'seq', axis=3, tiled=True)  86.4 us
    all_gather x2, blocking collectives, per_device(): lax.all_gather(row_delta, 'seq', axis=3, tiled=True)  66.1 us
    unnamed x1, blocking collectives  58.8 us
    all_gather x2, blocking collectives, gather_keys(): lax.all_gather(value_low, 'seq', axis=1, tiled=True)  54.8 us
    all_gather x2, blocking collectives, gather_keys(): lax.all_gather(key_low, 'seq', axis=1, tiled=True)  45.6 us
    unnamed x282, local copies, waits for them, and re-layouts  44.9 us
  transfers between devices with their start and end apart: 23, of which 13 were waited for; matrix products, arithmetic and copies ran while one was open for 26% of the time, Pallas kernels for 0%

profile of v1, /device:TPU:0, one launch (start us, length us, event | category | flops | bytes accessed | tf_op | source)
XLA Modules:
  0.0 1193.4 jit_solution(14533990156027541795)
XLA Ops:
  7.3 6.7 all-gather.13
  15.0 5.4 all-gather.15
  21.5 6.7 all_gather.103
  28.3 7.2 all_gather.105
  35.6 7.4 all-gather.16
  50.3 4.6 all-gather.12
  55.1 26.0 %all_gather.93 = bf16[1152,384]{1,0:T(8,128)(2,1)S(1)} all-gather(bf16[72,384]{1,0:T(8,128)(2,1)S(1)} %bitcast.944), channel_id=1, replica_groups=mesh['dp'=2,'seq'=16] {'seq'}, dimensions={0}, use_global_device_ids=true | all-gather | bytes 940032 | tf_op jit(solution)/shard_map/all_gather | solution.py:76
  81.9 58.8 %all-reduce.9 = (bf16[1024]{0:T(1024)(128)(2,1)S(1)}, bf16[1152]{0:T(1024)(128)(2,1)S(1)}, bf16[1152]{0:T(1024)(128)(2,1)S(1)}, bf16[1024]{0:T(1024)(128)(2,1)S(1)}) all-reduce(bf16[1024]{0:T(1024)(128)(2,1)S(1)} %dynamic-update-slice.3, bf16[1152]{0:T(1024)(128)(2,1)S(1)} %dynamic-update-slice.1, ...), channel_id=5, replica_groups=mesh['dp'=2,'seq'=16] {'seq'}, use_global_device_ids=true, to_apply=%add.3 | all-reduce | flops 4352 | bytes 17408
  142.1 4.6 all-gather.14
  146.9 23.9 %all_gather.98 = bf16[1152,384]{1,0:T(8,128)(2,1)S(1)} all-gather(bf16[72,384]{1,0:T(8,128)(2,1)S(1)} %bitcast.945), channel_id=1, replica_groups=mesh['dp'=2,'seq'=16] {'seq'}, dimensions={0}, use_global_device_ids=true | all-gather | bytes 940032 | tf_op jit(solution)/shard_map/all_gather | solution.py:77
  175.0 20.4 %all-gather.4 = bf16[1024,384]{1,0:T(8,128)(2,1)S(1)} all-gather(bf16[64,384]{1,0:T(8,128)(2,1)S(1)} %get-tuple-element.1293), channel_id=6, replica_groups=mesh['dp'=2,'seq'=16] {'seq'}, dimensions={0}, use_global_device_ids=true | all-gather | bytes 835584 | tf_op jit(solution)/shard_map/all_gather | solution.py:89
  195.7 23.5 %all-gather.5 = bf16[1024,384]{1,0:T(8,128)(2,1)S(1)} all-gather(bf16[64,384]{1,0:T(8,128)(2,1)S(1)} %convolution_convert_fusion.2), channel_id=7, replica_groups=mesh['dp'=2,'seq'=16] {'seq'}, dimensions={0}, use_global_device_ids=true | all-gather | bytes 835584 | tf_op jit(solution)/shard_map/all_gather | solution.py:90
  219.5 25.2 %all-gather.1 = bf16[1024,384]{1,0:T(8,128)(2,1)S(1)} all-gather(bf16[64,384]{1,0:T(8,128)(2,1)S(1)} %get-tuple-element.1292), channel_id=3, replica_groups=mesh['dp'=2,'seq'=16] {'seq'}, dimensions={0}, use_global_device_ids=true | all-gather | bytes 835584 | tf_op jit(solution)/shard_map/all_gather | solution.py:89
  245.9 31.3 %all-gather.2 = bf16[1024,384]{1,0:T(8,128)(2,1)S(1)} all-gather(bf16[64,384]{1,0:T(8,128)(2,1)S(1)} %convolution_convert_fusion.3), channel_id=4, replica_groups=mesh['dp'=2,'seq'=16] {'seq'}, dimensions={0}, use_global_device_ids=true | all-gather | bytes 835584 | tf_op jit(solution)/shard_map/all_gather | solution.py:90
  301.7 3.9 fusion.170
  316.3 4.2 while.96
  322.5 4.9 while.97
  342.2 5.3 fusion.254
  347.5 5.3 fusion.255
  352.8 5.8 multiply_convert_fusion.2
  358.7 5.8 fusion.259
  396.8 8.0 while.100
  405.8 7.5 while.102
  428.3 59.4 %all_gather.113 = f32[1,6,3,1024]{1,0,2,3:T(1,128)S(1)} all-gather(f32[1,6,3,64]{1,0,2,3:T(1,128)S(1)} %copy-done.86), channel_id=1, replica_groups=mesh['dp'=2,'seq'=16] {'seq'}, dimensions={3}, use_global_device_ids=true | all-gather | bytes 78336 | tf_op jit(solution)/shard_map/all_gather | solution.py:436
  490.8 26.9 %all_gather.117 = f32[1,6,3,1024]{1,0,2,3:T(1,128)S(1)} all-gather(f32[1,6,3,64]{1,0,2,3:T(1,128)S(1)} %copy-done.84), channel_id=1, replica_groups=mesh['dp'=2,'seq'=16] {'seq'}, dimensions={3}, use_global_device_ids=true | all-gather | bytes 78336 | tf_op jit(solution)/shard_map/all_gather | solution.py:436
  521.8 32.5 %all-gather.8 = f32[6,3,1024]{0,1,2:T(4,128)S(1)} all-gather(f32[6,3,64]{0,1,2:T(4,128)S(1)} %copy.206), channel_id=10, replica_groups=mesh['dp'=2,'seq'=16] {'seq'}, dimensions={2}, use_global_device_ids=true | all-gather | bytes 78336 | tf_op jit(solution)/shard_map/all_gather | solution.py:437
  555.8 33.6 %all-gather.11 = f32[6,3,1024]{0,1,2:T(4,128)S(1)} all-gather(f32[6,3,64]{0,1,2:T(4,128)S(1)} %copy.224), channel_id=13, replica_groups=mesh['dp'=2,'seq'=16] {'seq'}, dimensions={2}, use_global_device_ids=true | all-gather | bytes 78336 | tf_op jit(solution)/shard_map/all_gather | solution.py:437
  595.8 27.9 %while.101 = (s32[]{:T(128)}, f32[1,64,6,64]{1,3,2,0:T(8,128)}, f32[1,64,6,64]{1,3,2,0:T(8,128)}, bf16[1,1024,1152]{2,1,0:T(8,128)(2,1)}, bf16[1,1024]{1,0:T(2,1...) while((s32[]{:T(128)}, f32[1,64,6,64]{1,3,2,0:T(8,128)}, ...), condition=%wide.region_21.22_spmd.clone, body=%wide.region_20.21_spmd.clone.sunk | while | flops 307446848 | bytes 26740732 | solution.py:283
  625.0 26.4 %while.103 = (s32[]{:T(128)}, f32[1,64,6,64]{1,3,2,0:T(8,128)}, f32[1,64,6,64]{1,3,2,0:T(8,128)}, bf16[1,1024,1152]{2,1,0:T(8,128)(2,1)}, bf16[1,1024]{1,0:T(2,1...) while((s32[]{:T(128)}, f32[1,64,6,64]{1,3,2,0:T(8,128)}, ...), condition=%wide.region_28.29_spmd.clone, body=%wide.region_27.28_spmd.clone.sunk | while | flops 307446848 | bytes 27331664 | solution.py:283
  662.6 7.0 fusion.212
  669.6 14.0 %reduce-scatter.59.cloned.1.call-done = bf16[72,1152]{1,0:T(8,128)(2,1)} async-done(((bf16[1152,1152]{1,0:T(8,128)(2,1)}), bf16[72,1152]{1,0:T(8,128)(2,1)}) %reduce-scatter.59.cloned.1.call-update) | async-done | bytes 165904
  685.5 10.0 fusion.144
  698.6 4.9 fusion.142
  706.5 4.9 fusion.143
  727.4 14.7 %reduce-scatter.55.cloned.1.call-done = bf16[72,384]{1,0:T(8,128)(2,1)} async-done(((bf16[1152,384]{1,0:T(8,128)(2,1)}), bf16[72,384]{1,0:T(8,128)(2,1)}) %reduce-scatter.55.cloned.1.call-update) | async-done | bytes 55312
  746.9 54.0 %reduce-scatter.57.cloned.1.call-done = bf16[72,384]{1,0:T(8,128)(2,1)} async-done(((bf16[1152,384]{1,0:T(8,128)(2,1)}), bf16[72,384]{1,0:T(8,128)(2,1)}) %reduce-scatter.57.cloned.1.call-update) | async-done | bytes 55312
  802.5 5.1 maximum_add_fusion.1
  807.7 6.4 reduce-scatter.43.cloned.1.call-done
  815.8 12.4 %reduce-scatter.49.cloned.1.call-done = bf16[576,72]{1,0:T(8,128)(2,1)} async-done(((bf16[1152,72]{1,0:T(8,128)(2,1)}), bf16[576,72]{1,0:T(8,128)(2,1)}) %reduce-scatter.49.cloned.1.call-update) | async-done | bytes 82960
  830.0 92.2 %reduce-scatter.41.cloned.1.call-done = bf16[192,1152]{1,0:T(8,128)(2,1)} async-done(((bf16[3072,1152]{1,0:T(8,128)(2,1)}), bf16[192,1152]{1,0:T(8,128)(2,1)}) %reduce-scatter.41.cloned.1.call-update) | async-done | bytes 442384 | tf_op jit(solution)/shard_map/reduce_scatter | solution.py:97
  926.5 89.7 %reduce-scatter.33.cloned.1.call-done = bf16[72,3072]{1,0:T(8,128)(2,1)} async-done(((bf16[1152,3072]{1,0:T(8,128)(2,1)}), bf16[72,3072]{1,0:T(8,128)(2,1)}) %reduce-scatter.33.cloned.1.call-update) | async-done | bytes 442384 | tf_op jit(solution)/shard_map/reduce_scatter | solution.py:97
  1016.3 40.5 %all-reduce.8 = (f32[2,1152]{1,0:T(2,128)S(1)}, f32[4]{0:T(128)S(1)}) all-reduce(f32[2,1152]{1,0:T(2,128)S(1)} %maximum_add_fusion, f32[4]{0:T(128)S(1)} %maximum_add_fusion.1), channel_id=1, replica_groups=mesh['dp'=2,'seq'=16] {'dp','seq'}, use_global_device_ids=true, to_apply=%region_48.49 | all-reduce | flops 2308 | bytes 18464 | tf_op jit(solution)/shard_map/psum | solution.py:494
  1058.6 51.5 %reduce-scatter.37.cloned.1.call-done = bf16[72,3072]{1,0:T(8,128)(2,1)} async-done(((bf16[1152,3072]{1,0:T(8,128)(2,1)}), bf16[72,3072]{1,0:T(8,128)(2,1)}) %reduce-scatter.37.cloned.1.call-update) | async-done | bytes 442384 | tf_op jit(solution)/shard_map/reduce_scatter | solution.py:97
  1111.7 10.8 reduce-scatter.45.cloned.1.call-done
  1124.0 11.2 reduce-scatter.47.cloned.1.call-done
  1136.7 16.1 %reduce-scatter.51.cloned.1.call-done = bf16[576,192]{1,0:T(8,128)(2,1)} async-done(((bf16[1152,192]{1,0:T(8,128)(2,1)}), bf16[576,192]{1,0:T(8,128)(2,1)}) %reduce-scatter.51.cloned.1.call-update) | async-done | bytes 221200
  1154.8 14.0 %reduce-scatter.35.cloned.1.call-done = bf16[72,1536]{1,0:T(8,128)(2,1)} async-done(((bf16[72,3072]{1,0:T(8,128)(2,1)}), bf16[72,1536]{1,0:T(8,128)(2,1)}) %reduce-scatter.35.cloned.1.call-update) | async-done | bytes 221200 | tf_op jit(solution)/shard_map/reduce_scatter | solution.py:101
  1170.6 14.3 %reduce-scatter.39.cloned.1.call-done = bf16[72,1536]{1,0:T(8,128)(2,1)} async-done(((bf16[72,3072]{1,0:T(8,128)(2,1)}), bf16[72,1536]{1,0:T(8,128)(2,1)}) %reduce-scatter.39.cloned.1.call-update) | async-done | bytes 221200 | tf_op jit(solution)/shard_map/reduce_scatter | solution.py:101
  (625 shorter events, 270.3 us)
Async XLA Ops:
  7.2 273.1 %all-gather.27.cloned.1.call-start = ((), (), s32[]{:S(2)}) async-start(), calls=%async_computation.14 | async-start | bytes 2820096 | tf_op jit(solution)/shard_map/all_gather | solution.py:75
  14.9 321.8 %all-gather.29.cloned.1.call-start = ((), (), s32[]{:S(2)}) async-start(), calls=%async_computation.15 | async-start | bytes 2820096 | tf_op jit(solution)/shard_map/all_gather | solution.py:78
  21.4 320.8 %all-gather.31.cloned.1.call-start = ((), (), s32[]{:S(2)}) async-start(), calls=%async_computation.16 | async-start | bytes 7520256 | tf_op jit(solution)/shard_map/all_gather | solution.py:79
  28.2 319.3 %all-gather.33.cloned.1.call-start = ((), (), s32[]{:S(2)}) async-start(), calls=%async_computation.17 | async-start | bytes 7520256 | tf_op jit(solution)/shard_map/all_gather | solution.py:80
  35.5 45.6 %copy-start.118 = (bf16[72]{0:T(256)(128)(2,1)S(1)}, bf16[72]{0:T(256)(128)(2,1)}, u32[]{:S(2)}) copy-start(bf16[72]{0:T(256)(128)(2,1)} %param.37) | copy-start | bytes 436
  35.5 45.8 %copy-start.119 = (bf16[72]{0:T(256)(128)(2,1)S(1)}, bf16[72]{0:T(256)(128)(2,1)}, u32[]{:S(2)}) copy-start(bf16[72]{0:T(256)(128)(2,1)} %param.38) | copy-start | bytes 436
  35.5 105.2 %copy-start.8 = (bf16[2,1,64,1152]{3,2,1,0:T(8,128)(2,1)S(1)}, bf16[2,1,64,1152]{3,2,1,0:T(8,128)(2,1)}, u32[]{:S(2)}) copy-start(bf16[2,1,64,1152]{3,2,1,0:T(8,128)(2,1)} %param.28) | copy-start | bytes 884740
  35.5 317.3 %all-gather.35.cloned.1.call-start = ((), (), s32[]{:S(2)}) async-start(), calls=%async_computation.18 | async-start | bytes 7520256 | tf_op jit(solution)/shard_map/all_gather | solution.py:81
  44.6 97.5 %copy-start.110 = (bf16[72,192]{1,0:T(8,128)(2,1)S(1)}, bf16[72,192]{1,0:T(8,128)(2,1)}, u32[]{:S(2)}) copy-start(bf16[72,192]{1,0:T(8,128)(2,1)} %param.32) | copy-start | bytes 82948
  44.7 549.7 %all-gather.37.cloned.1.call-start = ((), (), s32[]{:S(2)}) async-start(), calls=%async_computation.24 | async-start | bytes 2506752 | tf_op jit(solution)/shard_map/all_gather | solution.py:432
  81.0 90.1 %copy-start.13 = (bf16[1152,384]{1,0:T(8,128)(2,1)}, bf16[1152,384]{1,0:T(8,128)(2,1)S(1)}, u32[]{:S(2)}) copy-start(bf16[1152,384]{1,0:T(8,128)(2,1)S(1)} %all_gather.93) | copy-start | bytes 2654212
  141.5 138.8 %copy-start.106 = (f32[64]{0:T(128)}, f32[64]{0:T(128)S(1)}, u32[]{:S(2)}) copy-start(f32[64]{0:T(128)S(1)} %get-tuple-element.1331) | copy-start | bytes 772
  141.5 143.5 %copy-start.103 = (f32[64]{0:T(128)}, f32[64]{0:T(128)S(1)}, u32[]{:S(2)}) copy-start(f32[64]{0:T(128)S(1)} %get-tuple-element.1320) | copy-start | bytes 772
  172.1 73.8 %copy-start.91 = (bf16[64,384]{1,0:T(8,128)(2,1)}, bf16[64,384]{1,0:T(8,128)(2,1)S(1)}, u32[]{:S(2)}) copy-start(bf16[64,384]{1,0:T(8,128)(2,1)S(1)} %convolution_convert_fusion.3) | copy-start | bytes 147460
  173.2 128.5 %copy-start.48 = (f32[64,64]{1,0:T(8,128)}, f32[64,64]{1,0:T(8,128)S(1)}, u32[]{:S(2)}) copy-start(f32[64,64]{1,0:T(8,128)S(1)} %get-tuple-element.1306) | copy-start | bytes 49156
  173.2 128.5 %copy-start.51 = (f32[64,64]{1,0:T(8,128)}, f32[64,64]{1,0:T(8,128)S(1)}, u32[]{:S(2)}) copy-start(f32[64,64]{1,0:T(8,128)S(1)} %get-tuple-element.1307) | copy-start | bytes 49156
  341.6 252.7 %all-gather.39.cloned.1.call-start = ((), (), s32[]{:S(2)}) async-start(), calls=%async_computation.25 | async-start | bytes 2506752 | tf_op jit(solution)/shard_map/all_gather | solution.py:433
  384.9 238.7 %all-gather.41.cloned.1.call-start = ((), (), s32[]{:S(2)}) async-start(), calls=%async_computation.26 | async-start | bytes 2506752 | tf_op jit(solution)/shard_map/all_gather | solution.py:432
  385.7 238.0 %all-gather.43.cloned.1.call-start = ((), (), s32[]{:S(2)}) async-start(), calls=%async_computation.27 | async-start | bytes 2506752 | tf_op jit(solution)/shard_map/all_gather | solution.py:433
  404.8 255.8 %reduce-scatter.53.cloned.1.call-start = ((), (), s32[]{:S(2)}) async-start(), calls=%async_computation.33 | async-start | bytes 2820096
  423.0 67.9 %copy-start.84 = (f32[1,6,3,64]{1,0,2,3:T(1,128)S(1)}, f32[1,6,3,64]{1,0,2,3:T(1,128)}, u32[]{:S(2)}) copy-start(f32[1,6,3,64]{1,0,2,3:T(1,128)} %copy-done.83) | copy-start | bytes 13828
  423.0 260.6 %reduce-scatter.59.cloned.1.call-start = ((), (), s32[]{:S(2)}) async-start(), calls=%async_computation.36 | async-start | bytes 2820096
  487.8 33.6 %copy-start.47 = (f32[6,3,64]{1,0,2:T(8,128)S(1)}, f32[6,3,64]{1,0,2:T(8,128)}, u32[]{:S(2)}) copy-start(f32[6,3,64]{1,0,2:T(8,128)} %copy-done.46) | copy-start | bytes 13828
  555.8 35.0 %copy-start.26 = (f32[64,1152]{1,0:T(8,128)S(1)}, f32[64,1152]{1,0:T(8,128)}, u32[]{:S(2)}) copy-start(f32[64,1152]{1,0:T(8,128)} %copy-done.25) | copy-start | bytes 884740
  555.8 35.0 %copy-start.62 = (bf16[64,1152]{1,0:T(8,128)(2,1)S(1)}, bf16[64,1152]{1,0:T(8,128)(2,1)}, u32[]{:S(2)}) copy-start(bf16[64,1152]{1,0:T(8,128)(2,1)} %copy-done.61) | copy-start | bytes 442372
  594.3 147.8 %reduce-scatter.55.cloned.1.call-start = ((), (), s32[]{:S(2)}) async-start(), calls=%async_computation.34 | async-start | bytes 940032
  657.8 143.1 %reduce-scatter.57.cloned.1.call-start = ((), (), s32[]{:S(2)}) async-start(), calls=%async_computation.35 | async-start | bytes 940032
  660.6 153.5 %reduce-scatter.43.cloned.1.call-start = ((), (), s32[]{:S(2)}) async-start(), calls=%async_computation.28 | async-start | bytes 442368
  662.5 165.7 %reduce-scatter.49.cloned.1.call-start = ((), (), s32[]{:S(2)}) async-start(), calls=%async_computation.31 | async-start | bytes 442368
  685.4 236.8 %reduce-scatter.41.cloned.1.call-start = ((), (), s32[]{:S(2)}) async-start(), calls=%async_computation.23 | async-start | bytes 7520256 | tf_op jit(solution)/shard_map/reduce_scatter | solution.py:97
  695.5 320.7 %reduce-scatter.33.cloned.1.call-start = ((), (), s32[]{:S(2)}) async-start(), calls=%async_computation.19 | async-start | bytes 7520256 | tf_op jit(solution)/shard_map/reduce_scatter | solution.py:97
  703.5 406.6 %reduce-scatter.37.cloned.1.call-start = ((), (), s32[]{:S(2)}) async-start(), calls=%async_computation.21 | async-start | bytes 7520256 | tf_op jit(solution)/shard_map/reduce_scatter | solution.py:97
  711.5 411.0 %reduce-scatter.45.cloned.1.call-start = ((), (), s32[]{:S(2)}) async-start(), calls=%async_computation.29 | async-start | bytes 147456
  727.4 197.2 %copy-start.14 = (bf16[1152,384]{1,0:T(8,128)(2,1)S(1)}, bf16[1152,384]{1,0:T(8,128)(2,1)}, u32[]{:S(2)}) copy-start(bf16[1152,384]{1,0:T(8,128)(2,1)} %copy-done.13) | copy-start | bytes 2654212
  727.4 197.2 %copy-start.72 = (f32[64,1152]{1,0:T(8,128)S(1)}, f32[64,1152]{1,0:T(8,128)}, u32[]{:S(2)}) copy-start(f32[64,1152]{1,0:T(8,128)} %fusion.204) | copy-start | bytes 884740
  727.4 197.2 %copy-start.96 = (bf16[64,384]{1,0:T(8,128)(2,1)S(1)}, bf16[64,384]{1,0:T(8,128)(2,1)}, u32[]{:S(2)}) copy-start(bf16[64,384]{1,0:T(8,128)(2,1)} %copy-done.95) | copy-start | bytes 147460
  743.7 391.5 %reduce-scatter.47.cloned.1.call-start = ((), (), s32[]{:S(2)}) async-start(), calls=%async_computation.30 | async-start | bytes 147456
  745.4 179.6 %copy-start.71 = (f32[64,1152]{1,0:T(8,128)S(1)}, f32[64,1152]{1,0:T(8,128)}, u32[]{:S(2)}) copy-start(f32[64,1152]{1,0:T(8,128)} %fusion.203) | copy-start | bytes 884740
  745.4 179.6 %copy-start.94 = (bf16[64,384]{1,0:T(8,128)(2,1)S(1)}, bf16[64,384]{1,0:T(8,128)(2,1)}, u32[]{:S(2)}) copy-start(bf16[64,384]{1,0:T(8,128)(2,1)} %copy-done.93) | copy-start | bytes 147460
  802.5 350.4 %reduce-scatter.51.cloned.1.call-start = ((), (), s32[]{:S(2)}) async-start(), calls=%async_computation.32 | async-start | bytes 884736
  830.0 95.5 %copy-start.12 = (bf16[1152,384]{1,0:T(8,128)(2,1)S(1)}, bf16[1152,384]{1,0:T(8,128)(2,1)}, u32[]{:S(2)}) copy-start(bf16[1152,384]{1,0:T(8,128)(2,1)} %copy-done.11) | copy-start | bytes 2654212
  830.0 95.5 %copy-start.82 = (bf16[1,64,6,64]{1,3,2,0:T(8,128)(2,1)S(1)}, bf16[1,64,6,64]{1,3,2,0:T(8,128)(2,1)}, u32[]{:S(2)}) copy-start(bf16[1,64,6,64]{1,3,2,0:T(8,128)(2,1)} %copy-done.81) | copy-start | bytes 147460
  924.3 244.5 %reduce-scatter.35.cloned.1.call-start = ((), (), s32[]{:S(2)}) async-start(), calls=%async_computation.20 | async-start | bytes 663552 | tf_op jit(solution)/shard_map/reduce_scatter | solution.py:101
  925.5 185.2 %copy-start.27 = (f32[64,1152]{1,0:T(8,128)S(1)}, f32[64,1152]{1,0:T(8,128)}, u32[]{:S(2)}) copy-start(f32[64,1152]{1,0:T(8,128)} %copy-done.25) | copy-start | bytes 884740
  925.5 185.2 %copy-start.30 = (f32[64,1152]{1,0:T(8,128)S(1)}, f32[64,1152]{1,0:T(8,128)}, u32[]{:S(2)}) copy-start(f32[64,1152]{1,0:T(8,128)} %copy-done.28) | copy-start | bytes 884740
  925.5 185.2 %copy-start.116 = (f32[64]{0:T(128)S(1)}, f32[64]{0:T(128)}, u32[]{:S(2)}) copy-start(f32[64]{0:T(128)} %get-tuple-element.1319) | copy-start | bytes 772
  925.5 185.2 %copy-start.117 = (f32[64]{0:T(128)S(1)}, f32[64]{0:T(128)}, u32[]{:S(2)}) copy-start(f32[64]{0:T(128)} %get-tuple-element.1332) | copy-start | bytes 772
  1016.2 168.7 %reduce-scatter.39.cloned.1.call-start = ((), (), s32[]{:S(2)}) async-start(), calls=%async_computation.22 | async-start | bytes 663552 | tf_op jit(solution)/shard_map/reduce_scatter | solution.py:101
  (105 other events, 495.8 us)
Sparse Core Ops, SparseCore 0:
  15.0 44.9 all-gather.26
  62.7 43.1 all-gather.28
  108.3 73.6 all-gather.30
  184.0 77.9 all-gather.32
  264.7 65.4 all-gather.34
  341.8 54.2 all-gather.36
  398.3 41.6 all-gather.38
  442.3 47.7 all-gather.40
  492.3 49.8 all-gather.42
  546.0 70.3 reduce-scatter.52
  620.8 62.7 reduce-scatter.58
  687.1 54.9 reduce-scatter.54
  745.7 55.1 reduce-scatter.56
  803.0 11.0 reduce-scatter.42
  816.2 12.0 reduce-scatter.48
  832.1 90.0 reduce-scatter.40
  926.6 89.5 reduce-scatter.32
  1020.0 90.0 reduce-scatter.36
  1113.0 9.4 reduce-scatter.44
  1125.2 9.9 reduce-scatter.46
  1137.6 15.2 reduce-scatter.50
  1155.1 13.6 reduce-scatter.34
  1171.2 13.6 reduce-scatter.38

commit v2 on v1

--- a/solution.py
+++ b/solution.py
@@ -1,8 +1,12 @@
+import functools
 import math
 
 import jax
 import jax.numpy as jnp
+import numpy as np
 from jax import lax
+from jax.experimental import pallas as pl
+from jax.experimental.pallas import tpu as pltpu
 from jax.sharding import PartitionSpec as P
 
 QUERY_HEADS = 18
@@ -513,6 +517,1336 @@
     )
 
 
+LANES = 128
+
+
+def fast_kernel(
+    meta_in,
+    x_in,
+    cot_in,
+    wq_in,
+    wo_in,
+    gu_in,
+    wd_in,
+    cos_in,
+    sin_in,
+    out_o,
+    gin_o,
+    gq_o,
+    go_o,
+    ggu_o,
+    gd_o,
+    small_o,
+    meta_r,
+    xo,
+    co,
+    n1g,
+    gfg,
+    n2g,
+    wq_r,
+    wq_w,
+    wo_r,
+    wo_w,
+    gu_r,
+    gu_w,
+    wd_r,
+    wd_w,
+    acc,
+    qk,
+    qt,
+    dat,
+    kw,
+    vw,
+    pb0,
+    pb1,
+    pb2,
+    pb3,
+    mx,
+    segr,
+    segc,
+    gains,
+    at_s,
+    at_r,
+    hid,
+    dhid,
+    inner_s,
+    dgu_s,
+    part_e,
+    e2r1,
+    e2r2,
+    bfr1,
+    bfr2,
+    da_s,
+    da_r,
+    d_s,
+    dkvt,
+    gux_r,
+    guz_r,
+    guf_r,
+    gd_s,
+    gdx_r,
+    gdz_r,
+    gor1,
+    gox_r,
+    goq_r,
+    goz_r,
+    gq_r,
+    small_s,
+    small_r,
+    rows_s,
+    rows_r,
+    ssem,
+    rsem,
+):
+    f32, bf16 = jnp.float32, jnp.bfloat16
+    part_f = n2g
+    e1r1, e1r2 = gfg.at[0], gfg.at[1]
+    x = lax.axis_index("dp")
+    s = lax.axis_index("seq")
+    zh, j = s // 8, s % 8
+    zl, y, c = j // 4, (j // 2) % 2, j % 2
+    own_chip = zl * 2 + y
+    attends = (j != 3) & (j != 5)
+
+    def head_of(device_index):
+        high = device_index // 4
+        return device_index - high * (1 + (device_index - 2) // 3)
+
+    head_own = head_of(j)
+    width = x_in.shape[2]
+    counter = [0]
+    pending = []
+
+    def index_of(mask):
+        return (
+            ((1 - zl) if mask & 4 else zl) * 4
+            + ((1 - y) if mask & 2 else y) * 2
+            + ((1 - c) if mask & 1 else c)
+        )
+
+    def device(mask=0, flip_x=False, flip_z=False):
+        return (
+            (1 - x) if flip_x else x,
+            ((1 - zh) if flip_z else zh) * 8 + index_of(mask),
+        )
+
+    def fresh():
+        counter[0] += 1
+        return counter[0] - 1
+
+    def send(src, dst, target, keep=True):
+        n = fresh()
+        copy = pltpu.make_async_remote_copy(
+            src_ref=src,
+            dst_ref=dst,
+            send_sem=ssem.at[n],
+            recv_sem=rsem.at[n],
+            device_id=target,
+            device_id_type=pl.DeviceIdType.MESH,
+        )
+        copy.start()
+        if keep:
+            pending.append(copy)
+        return copy
+
+    def mm(a, b):
+        return jnp.dot(a, b, preferred_element_type=f32)
+
+    def mm_t(a, b):
+        return lax.dot_general(a, b, (((1,), (1,)), ((), ())), preferred_element_type=f32)
+
+    def mm_w(a, b):
+        return lax.dot_general(a, b, (((0,), (0,)), ((), ())), preferred_element_type=f32)
+
+    chip_y, chip_z, chip_d = zl * 2 + 1 - y, (1 - zl) * 2 + y, (1 - zl) * 2 + 1 - y
+
+    class Gather:
+        def __init__(self, view, pair=True, halves=(True, True)):
+            self.view, self.pair, self.halves = view, pair, halves
+            self.copies, self.cores = [], []
+
+        def start(self, source=None):
+            own = self.view(own_chip)
+            source = own if source is None else source
+            self.z = self.put(source, own, 4)
+            self.y = self.put(source, own, 2)
+            if self.pair:
+                self.cores.append(self.put(source, own, 1))
+
+        def put(self, source, place, mask):
+            copy = send(source, place, device(mask))
+            self.copies.append(copy)
+            return copy
+
+        def part(self, chip, half):
+            view = self.view(chip)
+            return view if self.halves[0] != self.halves[1] else view.at[half]
+
+        def from_z(self):
+            self.z.wait_recv()
+            if self.halves[0]:
+                self.zy = self.put(self.part(chip_z, 0), self.part(chip_z, 0), 2)
+            if self.pair:
+                self.cores.append(self.put(self.view(chip_z), self.view(chip_z), 1))
+
+        def from_y(self):
+            self.y.wait_recv()
+            if self.halves[1]:
+                self.yz = self.put(self.part(chip_y, 1), self.part(chip_y, 1), 4)
+            if self.pair:
+                self.cores.append(self.put(self.view(chip_y), self.view(chip_y), 1))
+
+        def from_far(self):
+            if self.halves[0]:
+                self.zy.wait_recv()
+            if self.halves[1]:
+                self.yz.wait_recv()
+            if self.pair:
+                self.cores.append(self.put(self.view(chip_d), self.view(chip_d), 1))
+
+        def finish(self):
+            for copy in self.cores:
+                copy.wait_recv()
+
+        def sent(self):
+            for copy in self.copies:
+                copy.wait_send()
+
+    def tokens_of(half):
+        return lambda chip: n1g.at[half, chip, c]
+
+    x_a = Gather(tokens_of(zh), True, (True, False))
+    x_b = Gather(tokens_of(1 - zh), True, (False, True))
+    x_a.start(x_in.at[zh])
+    x_copy = send(x_in.at[1 - zh], n1g.at[zh, own_chip, c], device(0, False, True))
+    meta_copies = []
+    for mask in range(8):
+        for far in (False, True):
+            if mask or far:
+                meta_copies.append(send(meta_in, meta_r.at[s], device(mask, False, far)))
+
+    qkv_sem = fresh()
+    qkv_first = []
+    for far_x in (False, True):
+        for far_z in (False, True):
+            for piece in range(3):
+                n = fresh()
+                tx = (1 - x) if far_x else x
+                tz = (1 - zh) if far_z else zh
+                target = (tx, tz * 8 + 4 * x + piece + x * ((piece + 1) // 2))
+                copy = pltpu.make_async_remote_copy(
+                    src_ref=wq_in.at[piece],
+                    dst_ref=wq_r.at[s],
+                    send_sem=ssem.at[n],
+                    recv_sem=rsem.at[qkv_sem],
+                    device_id=target,
+                    device_id_type=pl.DeviceIdType.MESH,
+                )
+                if far_x or far_z:
+                    copy.start()
+                    pending.append(copy)
+                else:
+                    here = j == 4 * x + piece + x * ((piece + 1) // 2)
+                    local = pltpu.make_async_copy(
+                        wq_in.at[piece], wq_r.at[s], rsem.at[qkv_sem]
+                    )
+                    pl.when(here)(local.start)
+                    pl.when(jnp.logical_not(here))(copy.start)
+                    qkv_first.append((here, copy))
+    wo_z = send(wo_in, wo_r.at[x, zh, own_chip, c], device(0, False, True))
+    wo_r[x, zh, own_chip, c] = wo_in[...]
+    wd_r[x, zh] = wd_in[...]
+    gu_r[x, zh, j] = gu_in[j]
+    meta_r[s] = meta_in[...]
+    n1g[zh, own_chip, c] = x_in[zh]
+    xo[zh] = x_in[zh]
+    co[zh] = cot_in[zh]
+    gfg[zh, own_chip, c] = cot_in[zh]
+    da_s[...] = jnp.zeros(da_s.shape, bf16)
+    wd_w[...] = jnp.zeros(wd_w.shape, bf16)
+
+    def norm_rows(values, gain):
+        scale = lax.rsqrt(jnp.mean(values * values, axis=-1, keepdims=True) + EPS)
+        return values * scale * gain, scale
+
+    x_copy.wait_recv()
+    x_b.start()
+    xo[1 - zh] = n1g[1 - zh, own_chip, c]
+    x_a.from_z()
+    x_a.from_y()
+    for copy in meta_copies:
+        copy.wait_recv()
+    gain_rows = jnp.zeros((8, width), f32)
+    seg_rows = jnp.zeros((8, 1024), f32)
+    for slot in range(16):
+        piece = meta_r[slot]
+        wide = jnp.concatenate([piece, jnp.zeros((8, width - LANES), f32)], axis=1)
+        gain_rows = gain_rows + pltpu.roll(wide, 72 * slot, 1)
+        wide = jnp.concatenate([piece, jnp.zeros((8, 1024 - LANES), f32)], axis=1)
+        seg_rows = seg_rows + pltpu.roll(wide, 64 * slot, 1)
+    gains[...] = gain_rows
+    seg_own = jnp.where(zh == 0, seg_rows[2:3, :], seg_rows[3:4, :])
+    seg_wide = jnp.broadcast_to(seg_own, (8, 1024))
+    segr[...] = seg_wide
+    segc[...] = seg_wide.T
+
+    x_a.from_far()
+    x_b.from_z()
+    x_b.from_y()
+    x_b.from_far()
+
+    def wo_view(chip):
+        return wo_r.at[x, :, chip, c]
+
+    def gf_view(chip):
+        return gfg.at[:, chip, c]
+
+    def n2_view(chip):
+        return n2g.at[:, chip, c]
+
+    wo_z.wait_recv()
+    wo_q = Gather(wo_view, False)
+    wo_q.start()
+    wo_x = [send(wo_view(own_chip), wo_view(own_chip), device(0, True))]
+
+    def spread_rows(read, columns):
+        def step(slot, carry):
+            acc[pl.ds(pl.multiple_of(slot * 72, 8), 72), 0:columns] = read(slot).astype(f32)
+            return carry
+
+        lax.fori_loop(0, 16, step, 0)
+
+    def to_low(store, columns):
+        def step(block, carry):
+            at = pl.multiple_of(block * 128, 128)
+            store(at, acc[pl.ds(at, 128), 0:columns].astype(bf16))
+            return carry
+
+        lax.fori_loop(0, 9, step, 0)
+
+    def from_rows(store):
+        def step(slot, carry):
+            store(slot, pl.multiple_of(slot * 72, 8))
+            return carry
+
+        lax.fori_loop(0, 16, step, 0)
+
+
+    @pl.when(attends)
+    def _():
+        pltpu.make_async_copy(wq_r, wq_r, rsem.at[qkv_sem]).wait()
+        spread_rows(lambda slot: wq_r[slot], 384)
+
+        def store(at, value):
+            wq_w[pl.ds(at, 128), :] = value
+
+        to_low(store, 384)
+
+    x_a.finish()
+    x_b.finish()
+    x_a.sent()
+    x_b.sent()
+    cot_copy = send(cot_in.at[1 - zh], co.at[zh], device(0, False, True))
+    gu_first = []
+    for mask in range(1, 8):
+        gu_first.append(send(gu_in.at[index_of(mask)], gu_r.at[x, zh, j], device(mask)))
+    wd_z = send(wd_in, wd_r.at[x, zh], device(0, False, True))
+    wd_x = send(wd_in, wd_r.at[x, zh], device(0, True))
+
+    lane256 = lax.broadcasted_iota(jnp.int32, (1, 256), 1)
+    low_half = (lane256 % 64) < 32
+
+    def swap_half(values):
+        return jnp.where(low_half, pltpu.roll(values, 256 - 32, 1), pltpu.roll(values, 32, 1))
+
+    def tables(at, rows):
+        cosine = cos_in[pl.ds(at, rows), :]
+        sine = sin_in[pl.ds(at, rows), :]
+        return (
+            jnp.concatenate([cosine, cosine], axis=1),
+            jnp.concatenate([sine, sine], axis=1),
+        )
+
+    @pl.when(attends)
+    def _():
+        def step(block, carry):
+            at = pl.multiple_of(block * 256, 256)
+            rows = n1g[block // 2, pl.ds((block % 2) * 2, 2)].reshape(256, width)
+            rows, _ = norm_rows(rows.astype(f32), gains[0:1, :])
+            rows = rows.astype(bf16)
+            n1g[block // 2, pl.ds((block % 2) * 2, 2)] = rows.reshape(2, 2, 64, width)
+            raw = mm(rows, wq_w[...])
+            cosine, sine = tables(at, 256)
+            pair = raw[:, 0:256]
+            turned = pair * cosine + swap_half(pair) * sine
+            turned = turned.astype(bf16).astype(f32)
+            qk[pl.ds(at, 256), :] = turned.astype(bf16)
+            qt[:, pl.ds(at, 256)] = turned.T[0:192].astype(bf16)
+            values = raw[:, 256:384].astype(bf16).astype(f32)
+            values = jnp.concatenate([values, jnp.zeros((256, 128), f32)], axis=1)
+            for head in range(3):
+                mine = (lane256 // 64) == head
+                shift = (64 * (head + 1)) % 256
+                kw[head, pl.ds(at, 256), :] = jnp.where(
+                    mine, pltpu.roll(turned, shift, 1), 0.0
+                ).astype(bf16)
+                placed = pltpu.roll(values, 64 * head, 1) if head else values
+                vw[head, pl.ds(at, 256), :] = placed.astype(bf16)
+            return carry
+
+        lax.fori_loop(0, 4, step, 0)
+
+    pbs = (pb0, pb1, pb2, pb3)
+    scale = 1.0 / math.sqrt(HEAD_DIMENSION)
+
+    def attend_block(quarter):
+        length = 256 * (quarter + 1)
+
+        def step(sub, carry):
+            at = pl.multiple_of(quarter * 256 + sub * 128, 128)
+            query = qk[pl.ds(at, 128), :]
+            key_pos = lax.broadcasted_iota(jnp.int32, (128, length), 1)
+            row_pos = lax.broadcasted_iota(jnp.int32, (128, length), 0) + at
+            allowed = (segc[pl.ds(at, 128), 0:1] == segr[0:1, 0:length]) & (key_pos <= row_pos)
+            mixed = jnp.zeros((128, 256), f32)
+            for head in range(3):
+                scores = mm_t(query, kw[head, 0:length, :])
+                scores = jnp.where(allowed, scores * scale, NEGATIVE)
+                top = jnp.max(scores, axis=-1, keepdims=True)
+                weight = jnp.exp(scores - top)
+                weight = weight / jnp.sum(weight, axis=-1, keepdims=True)
+                low_p = weight.astype(bf16)
+                pbs[quarter][head, pl.ds(pl.multiple_of(sub * 128, 128), 128), :] = low_p
+                mixed = mixed + mm(low_p, vw[head, 0:length, :])
+            mx[pl.ds(at, 128), :] = mixed
+            at_s[quarter // 2, pl.ds((quarter % 2) * 4 + sub * 2, 2)] = mixed.astype(
+                bf16
+            ).reshape(2, 64, 256)
+            return carry
+
+        lax.fori_loop(0, 2, step, 0)
+
+    wo_q.from_z()
+    wo_x.append(send(wo_view(chip_z), wo_view(chip_z), device(0, True)))
+    pl.when(attends)(lambda: attend_block(0))
+    wo_q.from_y()
+    wo_x.append(send(wo_view(chip_y), wo_view(chip_y), device(0, True)))
+    pl.when(attends)(lambda: attend_block(1))
+    for copy in gu_first:
+        copy.wait_recv()
+    gu_z = []
+    for part in range(2):
+        rows = gu_r.at[x, zh, 4 * part : 4 * part + 4]
+        gu_z.append(send(rows, rows, device(0, False, True)))
+    gu_x = [send(gu_r.at[x, zh], gu_r.at[x, zh], device(0, True))]
+    pl.when(attends)(lambda: attend_block(2))
+    wo_q.from_far()
+    wo_x.append(send(wo_view(chip_d), wo_view(chip_d), device(0, True)))
+    wo_c = [send(wo_r.at[x, :, :, c], wo_r.at[x, :, :, c], device(1))]
+    pl.when(attends)(lambda: attend_block(3))
+
+    at_copies = []
+    for mask in range(1, 8):
+        n = fresh()
+        there = index_of(mask)
+        copy = pltpu.make_async_remote_copy(
+            src_ref=at_s.at[:, there],
+            dst_ref=at_r.at[head_own],
+            send_sem=ssem.at[n],
+            recv_sem=rsem.at[n],
+            device_id=device(mask),
+            device_id_type=pl.DeviceIdType.MESH,
+        )
+        pl.when(attends)(copy.start)
+        at_copies.append(((there != 3) & (there != 5), copy))
+
+    @pl.when(attends)
+    def _():
+        at_r[head_own] = at_s[:, j]
+
+    cot_copy.wait_recv()
+    gfg[1 - zh, own_chip, c] = co[1 - zh]
+    gf_all = Gather(gf_view)
+    gf_all.start()
+    for copy in wo_x:
+        copy.wait_recv()
+    wo_c.append(send(wo_r.at[1 - x, :, :, c], wo_r.at[1 - x, :, :, c], device(1)))
+    wd_z.wait_recv()
+    wd_f = send(wd_r.at[x, 1 - zh], wd_r.at[x, 1 - zh], device(0, True))
+    for copy in wo_c:
+        copy.wait_recv()
+
+    def spread_left(slot):
+        z_half, chip, core = slot // 8, (slot % 8) // 2, slot % 2
+        left = wo_r[0, z_half, chip, core].astype(f32)
+        right = wo_r[1, z_half, chip, core, :, 0:128].astype(f32)
+        return jnp.concatenate([left[:, 0:512], left[:, 512:640] + right], axis=1)
+
+    def store_left(at, value):
+        wo_w[pl.ds(at, 128), 0:640] = value
+
+    spread_rows(spread_left, 640)
+    to_low(store_left, 640)
+
+    def store_right(at, value):
+        wo_w[pl.ds(at, 128), 640:1152] = value
+
+    spread_rows(lambda slot: wo_r[1, slot // 8, (slot % 8) // 2, slot % 2, :, 128:640], 512)
+    to_low(store_right, 512)
+
+    for theirs, copy in at_copies:
+        pl.when(theirs)(copy.wait_recv)
+
+    def branch_of():
+        total = jnp.zeros((128, width), f32)
+        for head in range(6):
+            piece = at_r[head].reshape(128, 256)[:, 0:192]
+            total = total + mm(piece, wo_w[192 * head : 192 * head + 192, :])
+        return total
+
+    branch = branch_of()
+    valid = jnp.concatenate(
+        [
+            (segc[pl.ds(pl.multiple_of(64 * j, 64), 64), 0:1] != 0).astype(f32),
+            (segc[pl.ds(pl.multiple_of(512 + 64 * j, 64), 64), 0:1] != 0).astype(f32),
+        ],
+        axis=0,
+    )
+    lane1 = lax.broadcasted_iota(jnp.int32, (1, LANES), 1)
+    square_attn = jnp.sum(jnp.sum(valid * branch * branch, axis=0, keepdims=True), axis=1, keepdims=True)
+    count = jnp.sum(valid, axis=0, keepdims=True)
+    hidden = xo[...].reshape(128, width).astype(f32) + branch
+    hid[...] = hidden
+    normed, _ = norm_rows(hidden, gains[1:2, :])
+    n2g[:, own_chip, c] = normed.astype(bf16).reshape(2, 64, width)
+    n2_all = Gather(n2_view)
+    n2_all.start()
+    gf_all.from_z()
+    gf_all.from_y()
+    for part in range(2):
+        gu_z[part].wait_recv()
+        rows = gu_r.at[x, 1 - zh, 4 * part : 4 * part + 4]
+        gu_x.append(send(rows, rows, device(0, True)))
+    gf_all.from_far()
+    n2_all.from_z()
+    n2_all.from_y()
+
+    wd_x.wait_recv()
+    wd_f.wait_recv()
+    for copy in gu_x:
+        copy.wait_recv()
+    for chunk in range(2):
+        spread_rows(lambda slot: gu_r[chunk, slot // 8, slot % 8], 384)
+
+        def store_gu(at, value):
+            gu_w[chunk, pl.ds(at, 128), :] = value
+
+        to_low(store_gu, 384)
+        left, right = wd_r[0, chunk], wd_r[1, chunk]
+        wd_w[chunk, 0:192, 0:512] = left[:, 0:512]
+        wd_w[chunk, 0:192, 512:640] = (
+            left[:, 512:640].astype(f32) + right[:, 0:128].astype(f32)
+        ).astype(bf16)
+        wd_w[chunk, 0:192, 640:1152] = right[:, 128:640]
+    n2_all.from_far()
+    gf_all.finish()
+    n2_all.finish()
+
+    def chip_at(step):
+        return ((zl + step + 1) % 2) * 2 + (y + (3 - step) // 2) % 2
+
+    def pair_copy(ref, got, base, step):
+        chip = chip_at(step)
+        return pltpu.make_async_remote_copy(
+            src_ref=ref.at[:, chip, 1 - c],
+            dst_ref=got.at[step],
+            send_sem=ssem.at[base + step],
+            recv_sem=rsem.at[base + step],
+            device_id=device(1),
+            device_id_type=pl.DeviceIdType.MESH,
+        )
+
+    def side_copy(ref, got2, base, kind):
+        step, half, slot, mask = (
+            (0, 0, 0, 2),
+            (0, 1, 0, 4),
+            (1, 0, 1, 2),
+            (2, 1, 2, 4),
+            (1, 1, 1, 2),
+            (2, 0, 2, 4),
+        )[kind]
+        return pltpu.make_async_remote_copy(
+            src_ref=ref.at[half, chip_at(step), c],
+            dst_ref=got2.at[slot, half],
+            send_sem=ssem.at[base + 4 + kind],
+            recv_sem=rsem.at[base + 4 + kind],
+            device_id=device(mask),
+            device_id_type=pl.DeviceIdType.MESH,
+        )
+
+    def pair_sum(ref, got, step):
+        chip = chip_at(step)
+        return ref[:, chip, c].astype(f32) + got[step].astype(f32)
+
+    def scatter_side(ref, got, got2, base, step):
+        pair_copy(ref, got, base, step).wait_recv()
+        ref[:, chip_at(step), c] = pair_sum(ref, got, step).astype(bf16)
+        for kind in ((0, 1), (2,), (3,))[step]:
+            side_copy(ref, got2, base, kind).start()
+
+    def scatter_first(ref, got, got2, compute):
+        base = counter[0]
+        counter[0] += 10
+
+        def step_fn(step, carry):
+            chip = chip_at(step)
+            block = compute(chip).astype(bf16).reshape(2, 2, 64, width)
+            ref[:, chip] = block
+            pair_copy(ref, got, base, step).start()
+            for done in range(3):
+                pl.when(step == done + 1)(
+                    functools.partial(scatter_side, ref, got, got2, base, done)
+                )
+            return carry
+
+        lax.fori_loop(0, 4, step_fn, 0)
+        return base
+
+    def scatter_second(ref, got, got2, base):
+        for kind, step, half in ((5, 2, 0), (4, 1, 1)):
+            side_copy(ref, got2, base, half).wait_recv()
+            chip = chip_at(step)
+            total = ref[half, chip, c].astype(f32) + got2[0, half].astype(f32)
+            ref[half, chip, c] = total.astype(bf16)
+            side_copy(ref, got2, base, kind).start()
+
+    def scatter_finish(ref, got, got2, base):
+        pair_copy(ref, got, base, 3).wait_recv()
+        total = pair_sum(ref, got, 3)
+        for kind in (2, 3, 4, 5):
+            side_copy(ref, got2, base, kind).wait_recv()
+        total = total + got2[1].astype(f32) + got2[2].astype(f32)
+        return total.reshape(128, width)
+
+    def scatter_sent(ref, got, got2, base):
+        for step in range(4):
+            pair_copy(ref, got, base, step).wait_send()
+        for kind in range(6):
+            side_copy(ref, got2, base, kind).wait_send()
+
+    lane128 = lax.broadcasted_iota(jnp.int32, (1, LANES), 1)
+
+    def feed_block(chip):
+        rows = n2g[:, chip].reshape(256, width)
+        grads = gfg[:, chip].reshape(256, width)
+        total = jnp.zeros((256, width), f32)
+        for chunk in range(2):
+            both = mm(rows, gu_w[chunk])
+            d_inner = mm_t(grads, wd_w[chunk])
+            gate_a, mid, up_a = both[:, 0:128], both[:, 128:256], both[:, 256:384]
+            turned = pltpu.roll(mid, 64, 1)
+            pieces = []
+            for gate, up, back in (
+                (gate_a, up_a, d_inner[:, 0:128]),
+                (mid, turned, d_inner[:, 128:256]),
+            ):
+                sig = jax.nn.sigmoid(gate)
+                silu = gate * sig
+                pieces.append(
+                    (silu * up, back * silu, back * up * sig * (1.0 + gate * (1.0 - sig)))
+                )
+            inner_s[chunk, :, pl.ds(chip * 2, 2), :, 0:128] = (
+                pieces[0][0].astype(bf16).reshape(2, 2, 64, 128)
+            )
+            inner_s[chunk, :, pl.ds(chip * 2, 2), :, 128:256] = (
+                jnp.where(lane128 < 64, pieces[1][0], 0.0).astype(bf16).reshape(2, 2, 64, 128)
+            )
+            gate_low = jnp.where(lane128 < 64, pieces[1][2], 0.0)
+            up_low = jnp.where(lane128 < 64, pieces[1][1], 0.0)
+            middle = (gate_low + pltpu.roll(up_low, 64, 1)).astype(bf16)
+            d_both = jnp.concatenate(
+                [pieces[0][2].astype(bf16), middle, pieces[0][1].astype(bf16)], axis=1
+            )
+            dgu_s[chunk, :, pl.ds(chip * 2, 2)] = d_both.reshape(2, 2, 64, 384)
+            total = total + mm_t(d_both, gu_w[chunk])
+        return total
+
+    e2_base = scatter_first(part_e, e2r1, e2r2, feed_block)
+    scatter_second(part_e, e2r1, e2r2, e2_base)
+
+    for copy in gu_x + gu_z:
+        copy.wait_send()
+    gf_all.sent()
+    for chunk in range(2):
+        grads = dgu_s[chunk].reshape(1024, 384)
+
+        def wide_step(block, carry):
+            at = pl.multiple_of(block * 128, 128)
+            rows = n2g[:, :, :, :, pl.ds(at, 128)].reshape(1024, 128)
+            acc[pl.ds(at, 128), 0:384] = mm_w(rows, grads)
+            return carry
+
+        lax.fori_loop(0, 9, wide_step, 0)
+
+        def cut(slot, at):
+            gu_r[chunk, slot // 8, slot % 8] = acc[pl.ds(at, 72), 0:384].astype(bf16)
+
+        from_rows(cut)
+    ggu_x = send(gu_r.at[1 - x], gux_r, device(0, True))
+
+    def down_step(chunk, carry):
+        grads = gfg[...].reshape(1024, width)
+        piece = mm_w(inner_s[chunk].reshape(1024, 256), grads)
+        gd_s[chunk, 0] = piece[0:192, 0:640].astype(bf16)
+        gd_s[chunk, 1] = piece[0:192, 512:1152].astype(bf16)
+        return carry
+
+    lax.fori_loop(0, 2, down_step, 0)
+    ggd_x = send(gd_s.at[:, 1 - x], gdx_r, device(0, True))
+
+    def result_block(chip):
+        total = mm(
+            inner_s[0, :, pl.ds(chip * 2, 2)].reshape(256, 256), wd_w[0]
+        )
+        return total + mm(inner_s[1, :, pl.ds(chip * 2, 2)].reshape(256, 256), wd_w[1])
+
+    n2_all.sent()
+    bf_base = scatter_first(part_f, bfr1, bfr2, result_block)
+
+    e2 = scatter_finish(part_e, e2r1, e2r2, e2_base)
+    hidden = hid[...]
+    scale2 = lax.rsqrt(jnp.mean(hidden * hidden, axis=-1, keepdims=True) + EPS)
+    scaled = e2 * gains[1:2, :]
+    inner_mean = jnp.mean(scaled * hidden, axis=-1, keepdims=True)
+    gain_feed_row = jnp.sum(e2 * hidden * scale2, axis=0, keepdims=True)
+    d_hidden = (
+        co[...].reshape(128, width).astype(f32)
+        + scale2 * scaled
+        - hidden * (scale2 * scale2 * scale2) * inner_mean
+    )
+    dhid[...] = d_hidden
+    d_low = d_hidden.astype(bf16)
+    for head in range(6):
+        piece = mm_t(d_low, wo_w[192 * head : 192 * head + 192, :])
+        da_s[head, :, :, 0:192] = piece.astype(bf16).reshape(2, 64, 192)
+    da_copies = []
+    for mask in range(1, 8):
+        n = fresh()
+        there = index_of(mask)
+        copy = pltpu.make_async_remote_copy(
+            src_ref=da_s.at[head_of(there)],
+            dst_ref=da_r.at[:, j],
+            send_sem=ssem.at[n],
+            recv_sem=rsem.at[n],
+            device_id=device(mask),
+            device_id_type=pl.DeviceIdType.MESH,
+        )
+        pl.when((there != 3) & (there != 5))(copy.start)
+        da_copies.append(((there != 3) & (there != 5), copy))
+
+    @pl.when(attends)
+    def _():
+        da_r[:, j] = da_s[head_own]
+
+    for copy in wo_c + wo_x:
+        copy.wait_send()
+    wo_q.sent()
+    for plane in range(2):
+        for head in range(6):
+            piece = at_r[head].reshape(128, 256)[:, 0:192]
+            acc[192 * head : 192 * head + 192, :] = mm_w(
+                piece, d_low[:, 512 * plane : 512 * plane + 640]
+            )
+
+        def cut_out(slot, at):
+            wo_r[plane, slot // 8, (slot % 8) // 2, slot % 2] = acc[pl.ds(at, 72), :].astype(bf16)
+
+        from_rows(cut_out)
+    go_c = send(wo_r.at[:, :, :, 1 - c], gor1, device(1))
+
+    dkvt[...] = jnp.zeros(dkvt.shape, f32)
+    for _, copy in da_copies:
+        pl.when(attends)(copy.wait_recv)
+
+    @pl.when(attends)
+    def _():
+        def step(block, carry):
+            at = pl.multiple_of(block * 256, 256)
+            rows = da_r[block // 2, pl.ds((block % 2) * 4, 4)].reshape(256, 256)
+            dat[:, pl.ds(at, 256)] = rows.astype(f32).T[0:192].astype(bf16)
+            return carry
+
+        lax.fori_loop(0, 4, step, 0)
+
+    def back_block(quarter):
+        length = 256 * (quarter + 1)
+
+        def step(sub, carry):
+            at = pl.multiple_of(quarter * 256 + sub * 128, 128)
+            grads = da_r[quarter // 2, pl.ds((quarter % 2) * 4 + sub * 2, 2)].reshape(128, 256)
+            products = grads.astype(f32) * mx[pl.ds(at, 128), :]
+            d_query = jnp.zeros((128, 256), f32)
+            d_key = jnp.zeros((64, length), f32)
+            d_value = jnp.zeros((64, length), f32)
+            for head in range(3):
+                delta = jnp.sum(
+                    jnp.where((lane256 // 64) == head, products, 0.0), axis=-1, keepdims=True
+                )
+                low_p = pbs[quarter][head, pl.ds(pl.multiple_of(sub * 128, 128), 128), :]
+                d_p = mm_t(grads, vw[head, 0:length, :])
+                d_s_low = (low_p.astype(f32) * (d_p - delta) * scale).astype(bf16)
+                d_query = d_query + mm(d_s_low, kw[head, 0:length, :])
+                d_key = d_key + mm(qt[64 * head : 64 * head + 64, pl.ds(at, 128)], d_s_low)
+                d_value = d_value + mm(dat[64 * head : 64 * head + 64, pl.ds(at, 128)], low_p)
+            mx[pl.ds(at, 128), :] = d_query
+            dkvt[0:64, 0:length] += d_value
+            dkvt[64:128, 0:length] += d_key
+            return carry
+
+        lax.fori_loop(0, 2, step, 0)
+
+    pl.when(attends)(lambda: back_block(0))
+    scatter_second(part_f, bfr1, bfr2, bf_base)
+    go_c.wait_recv()
+
+    def go_add(chip, carry):
+        for half in range(2):
+            for plane in range(2):
+                wo_r[plane, half, chip, c] = (
+                    wo_r[plane, half, chip, c].astype(f32) + gor1[plane, half, chip].astype(f32)
+                ).astype(bf16)
+        return carry
+
+    lax.fori_loop(0, 4, go_add, 0)
+
+    def go_side(chip, half, slot, mask):
+        return send(wo_r.at[:, half, chip, c], goq_r.at[slot, half], device(mask))
+
+    def go_sum(half, chip, slot):
+        for plane in range(2):
+            wo_r[plane, half, chip, c] = (
+                wo_r[plane, half, chip, c].astype(f32) + goq_r[slot, half, plane].astype(f32)
+            ).astype(bf16)
+
+    go_first = [
+        go_side(chip_d, 0, 0, 2),
+        go_side(chip_d, 1, 0, 4),
+        go_side(chip_y, 0, 1, 2),
+        go_side(chip_z, 1, 2, 4),
+    ]
+    pl.when(attends)(lambda: back_block(1))
+    ggu_x.wait_recv()
+
+    def gu_add(slot, carry):
+        gu_r[x, slot // 8, slot % 8] = (
+            gu_r[x, slot // 8, slot % 8].astype(f32) + gux_r[slot // 8, slot % 8].astype(f32)
+        ).astype(bf16)
+        return carry
+
+    lax.fori_loop(0, 16, gu_add, 0)
+    ggu_z = send(gu_r.at[x, 1 - zh], guz_r, device(0, False, True))
+    pl.when(attends)(lambda: back_block(2))
+    pl.when(attends)(lambda: back_block(3))
+
+    @pl.when(attends)
+    def _():
+        def step(block, carry):
+            at = pl.multiple_of(block * 256, 256)
+            cosine, sine = tables(at, 256)
+            turned = dkvt[:, pl.ds(at, 256)].T
+            query = mx[pl.ds(at, 256), :]
+            pair = jnp.concatenate(
+                [query[:, 0:128], jnp.where(lane128 < 64, query[:, 128:256], turned)], axis=1
+            )
+            back = pair * cosine - swap_half(pair) * sine
+            values = jnp.where(lane128 < 64, turned, 0.0)
+            both = jnp.concatenate([back.astype(bf16), values.astype(bf16)], axis=1)
+            d_s[block // 2, pl.ds((block % 2) * 4, 4)] = both.reshape(4, 64, 384)
+            return carry
+
+        lax.fori_loop(0, 4, step, 0)
+
+    @pl.when(jnp.logical_not(attends))
+    def _():
+        d_s[...] = jnp.zeros(d_s.shape, bf16)
+        wq_w[...] = jnp.zeros(wq_w.shape, bf16)
+
+    def input_block(chip):
+        return mm_t(d_s[:, pl.ds(chip * 2, 2)].reshape(256, 384), wq_w[...])
+
+    scatter_sent(part_e, e2r1, e2r2, e2_base)
+    e1_base = scatter_first(part_e, e1r1, e1r2, input_block)
+    scatter_second(part_e, e1r1, e1r2, e1_base)
+
+    ggd_x.wait_recv()
+    for half in range(2):
+        gd_s[half, x] = (gd_s[half, x].astype(f32) + gdx_r[half].astype(f32)).astype(bf16)
+    ggd_z = send(gd_s.at[1 - zh, x], gdz_r, device(0, False, True))
+    for n, half, chip, mask, slot in ((0, 0, chip_z, 4, 2), (1, 1, chip_y, 2, 1)):
+        go_first[n].wait_recv()
+        go_sum(half, chip, 0)
+        go_first.append(go_side(chip, half, slot, mask))
+
+    branch_feed = scatter_finish(part_f, bfr1, bfr2, bf_base)
+    result = hid[...] + branch_feed
+    square_feed = jnp.sum(
+        jnp.sum(valid * branch_feed * branch_feed, axis=0, keepdims=True), axis=1, keepdims=True
+    )
+    square_out = jnp.sum(
+        jnp.sum(valid * result * result, axis=0, keepdims=True), axis=1, keepdims=True
+    )
+    rows_s[0] = result.astype(bf16).reshape(2, 64, width)
+    ret_out = send(rows_s.at[0, 1 - zh], rows_r.at[0], device(0, False, True))
+    out_o[zh] = rows_s[0, zh]
+
+    gq_send, gq_sem = fresh(), fresh()
+    plane_to = zl
+    piece_own = head_own - 3 * zl
+
+    def gq_copy(slot):
+        return pltpu.make_async_remote_copy(
+            src_ref=wq_r.at[slot],
+            dst_ref=gq_r.at[x * 2 + zh, piece_own],
+            send_sem=ssem.at[gq_send],
+            recv_sem=rsem.at[gq_sem],
+            device_id=(plane_to, slot),
+            device_id_type=pl.DeviceIdType.MESH,
+        )
+
+    @pl.when(attends)
+    def _():
+        grads = d_s[...].reshape(1024, 384)
+
+        def wide_step(block, carry):
+            at = pl.multiple_of(block * 128, 128)
+            rows = n1g[:, :, :, :, pl.ds(at, 128)].reshape(1024, 128)
+            acc[pl.ds(at, 128), 0:384] = mm_w(rows, grads)
+            return carry
+
+        lax.fori_loop(0, 9, wide_step, 0)
+
+        def step(slot, carry):
+            wq_r[slot] = acc[pl.ds(pl.multiple_of(slot * 72, 8), 72), 0:384].astype(bf16)
+            here = (plane_to == x) & (slot == s)
+
+            @pl.when(here)
+            def _():
+                pltpu.make_async_copy(
+                    wq_r.at[slot], gq_r.at[x * 2 + zh, piece_own], rsem.at[gq_sem]
+                ).start()
+
+            pl.when(jnp.logical_not(here))(lambda: gq_copy(slot).start())
+            return carry
+
+        lax.fori_loop(0, 16, step, 0)
+
+    ggu_z.wait_recv()
+
+    def gu_add2(slot, carry):
+        gu_r[x, zh, slot] = (
+            gu_r[x, zh, slot].astype(f32) + guz_r[slot].astype(f32)
+        ).astype(bf16)
+        return carry
+
+    lax.fori_loop(0, 8, gu_add2, 0)
+    ggu_q = [
+        send(gu_r.at[x, zh, index_of(mask)], guf_r.at[j], device(mask)) for mask in range(1, 8)
+    ]
+    guf_r[j] = gu_r[x, zh, j]
+    e1 = scatter_finish(part_e, e1r1, e1r2, e1_base)
+    tokens = xo[...].reshape(128, width).astype(f32)
+    scale1 = lax.rsqrt(jnp.mean(tokens * tokens, axis=-1, keepdims=True) + EPS)
+    scaled = e1 * gains[0:1, :]
+    inner_mean = jnp.mean(scaled * tokens, axis=-1, keepdims=True)
+    gain_attn_row = jnp.sum(e1 * tokens * scale1, axis=0, keepdims=True)
+    grad_rows = (
+        dhid[...] + scale1 * scaled - tokens * (scale1 * scale1 * scale1) * inner_mean
+    )
+    rows_s[1] = grad_rows.astype(bf16).reshape(2, 64, width)
+    ret_in = send(rows_s.at[1, 1 - zh], rows_r.at[1], device(0, False, True))
+    gin_o[zh] = rows_s[1, zh]
+
+    total_row = jnp.where(
+        lane1 == 0,
+        square_attn,
+        jnp.where(lane1 == 1, square_feed, jnp.where(lane1 == 2, square_out, count)),
+    )
+    row8 = lax.broadcasted_iota(jnp.int32, (8, 1), 0)
+    both_gains = jnp.where(
+        row8 == 0,
+        jnp.broadcast_to(gain_attn_row, (8, width)),
+        jnp.broadcast_to(gain_feed_row, (8, width)),
+    )
+    for slot in range(16):
+        moved = pltpu.roll(both_gains, (width - 72 * slot) % width, 1) if slot else both_gains
+        small_s[slot] = jnp.where(row8 == 2, total_row, moved[:, 0:LANES])
+    small_copies = []
+    for flip_x in (False, True):
+        for flip_z in (False, True):
+            for mask in range(8):
+                if flip_x or flip_z or mask:
+                    target = device(mask, flip_x, flip_z)
+                    small_copies.append(
+                        send(small_s.at[target[1]], small_r.at[x * 16 + s], target)
+                    )
+    small_r[x * 16 + s] = small_s[s]
+
+    for copy in go_first[2:]:
+        copy.wait_recv()
+    for slot in (1, 2):
+        for half in range(2):
+            go_sum(half, own_chip, slot)
+    go_x = send(wo_r.at[1 - x, :, own_chip, c], gox_r, device(0, True))
+
+    go_x.wait_recv()
+    for half in range(2):
+        wo_r[x, half, own_chip, c] = (
+            wo_r[x, half, own_chip, c].astype(f32) + gox_r[half].astype(f32)
+        ).astype(bf16)
+    go_z = send(wo_r.at[x, 1 - zh, own_chip, c], goz_r, device(0, False, True))
+    ggd_z.wait_recv()
+    gd_o[...] = gd_s[zh, x].astype(f32) + gdz_r[...].astype(f32)
+    for copy in ggu_q:
+        copy.wait_recv()
+    ggu_o[...] = guf_r[...]
+    go_z.wait_recv()
+    go_o[...] = wo_r[x, zh, own_chip, c].astype(f32) + goz_r[...].astype(f32)
+    ret_out.wait_recv()
+    out_o[1 - zh] = rows_r[0]
+    pltpu.make_async_copy(gq_r, gq_r, rsem.at[gq_sem]).wait()
+    gq_o[...] = (
+        (gq_r[0].astype(f32) + gq_r[1].astype(f32)) + (gq_r[2].astype(f32) + gq_r[3].astype(f32))
+    )
+    for copy in small_copies:
+        copy.wait_recv()
+    total = small_r[0]
+    for slot in range(1, 32):
+        total = total + small_r[slot]
+    small_o[...] = total
+    ret_in.wait_recv()
+    gin_o[1 - zh] = rows_r[1]
+
+    waited = {id(copy) for copy in wo_c + wo_x + gu_x + gu_z}
+    for gather in (wo_q, gf_all, n2_all, x_a, x_b):
+        waited |= {id(copy) for copy in gather.copies}
+    for copy in pending:
+        if id(copy) not in waited:
+            copy.wait_send()
+    for here, copy in qkv_first:
+        pl.when(jnp.logical_not(here))(copy.wait_send)
+    for theirs, copy in at_copies:
+        pl.when(attends)(copy.wait_send)
+    for theirs, copy in da_copies:
+        pl.when(theirs)(copy.wait_send)
+    scatter_sent(part_f, bfr1, bfr2, bf_base)
+    scatter_sent(part_e, e1r1, e1r2, e1_base)
+
+    @pl.when(attends)
+    def _():
+        def step(slot, carry):
+            here = (plane_to == x) & (slot == s)
+            pl.when(jnp.logical_not(here))(lambda: gq_copy(slot).wait_send())
+            return carry
+
+        lax.fori_loop(0, 16, step, 0)
+
+
+def roll64(values):
+    return pltpu.roll(values, 64, 1)
+
+
+def prepare_kernel(
+    ga, gf, seg, wq, wk, wv, wo, gate, up, wd, meta_o, wq_o, wo_o, gu_o, wd_o
+):
+    f32, bf16 = jnp.float32, jnp.bfloat16
+    first = lax.axis_index("dp") == 0
+    rows = wq.shape[0]
+    low = lax.broadcasted_iota(jnp.int32, (1, LANES), 1) < 64
+    meta_o[...] = jnp.zeros(meta_o.shape, f32)
+    meta_o[0:1, 0:rows] = ga[...].astype(f32)
+    meta_o[1:2, 0:rows] = gf[...].astype(f32)
+    meta_o[2:4, 0:64] = seg[...].astype(f32)
+
+    def part(ref, at, size=LANES):
+        values = ref[:, at : at + size].astype(f32)
+        if size < LANES:
+            values = jnp.concatenate(
+                [values, jnp.zeros((values.shape[0], LANES - size), f32)], axis=1
+            )
+        return values
+
+    q = [part(wq, LANES * n) for n in range(4)] + [part(wq, 512, 64)]
+    k = [part(wk, 0), part(wk, LANES, 64)]
+    v = [part(wv, 0), part(wv, LANES, 64)]
+    slabs = (
+        (q[0], jnp.where(low, q[1], roll64(k[0])), jnp.where(low, v[0], 0.0)),
+        (
+            jnp.where(low, roll64(q[1]), roll64(q[2])),
+            jnp.where(low, roll64(q[2]), k[0]),
+            jnp.where(low, roll64(v[0]), 0.0),
+        ),
+        (q[3], jnp.where(low, q[4], roll64(k[1])), v[1]),
+    )
+    for head in range(3):
+        for place in range(3):
+            wq_o[head, :, LANES * place : LANES * (place + 1)] = slabs[head][place].astype(bf16)
+
+    def window(ref, out):
+        pieces = [part(ref, LANES * n) for n in range(4)] + [part(ref, 512, 64)]
+        before = jnp.zeros_like(pieces[0])
+        for n in range(5):
+            moved = jnp.where(low, roll64(before), roll64(pieces[n]))
+            out[:, LANES * n : LANES * (n + 1)] = jnp.where(first, pieces[n], moved).astype(bf16)
+            before = pieces[n]
+
+    window(wo, wo_o)
+    window(wd, wd_o)
+    for pair in range(4):
+        g = [part(gate, 384 * pair + LANES * n) for n in range(3)]
+        u = [part(up, 384 * pair + LANES * n) for n in range(3)]
+        slabs = (
+            (g[0], jnp.where(low, g[1], roll64(u[1])), u[0]),
+            (
+                jnp.where(low, roll64(g[1]), roll64(g[2])),
+                jnp.where(low, roll64(g[2]), u[2]),
+                jnp.where(low, roll64(u[1]), roll64(u[2])),
+            ),
+        )
+        for odd in range(2):
+            for place in range(3):
+                gu_o[2 * pair + odd, :, LANES * place : LANES * (place + 1)] = slabs[odd][
+                    place
+                ].astype(bf16)
+
+
+def finish_kernel(
+    out, gin, gq, go, ggu, gd, small,
+    out_o, gin_o, gq_o, gk_o, gv_o, go_o, gg_o, gu_o, gd_o, ga_o, gf_o, rm_o,
+):
+    f32 = jnp.float32
+    first = lax.axis_index("dp") == 0
+    rows = gq.shape[1]
+    low = lax.broadcasted_iota(jnp.int32, (1, LANES), 1) < 64
+    out_o[...] = out[...]
+    gin_o[...] = gin[...]
+    p = [[gq[head, :, LANES * n : LANES * (n + 1)].astype(f32) for n in range(3)] for head in range(3)]
+    gq_o[:, 0:128] = p[0][0]
+    gq_o[:, 128:256] = jnp.where(low, p[0][1], roll64(p[1][0]))
+    gq_o[:, 256:384] = jnp.where(low, roll64(p[1][0]), roll64(p[1][1]))
+    gq_o[:, 384:512] = p[2][0]
+    gq_o[:, 512:576] = p[2][1][:, 0:64]
+    gk_o[:, 0:128] = jnp.where(low, roll64(p[0][1]), p[1][1])
+    gk_o[:, 128:192] = roll64(p[2][1])[:, 0:64]
+    gv_o[:, 0:128] = jnp.where(low, p[0][2], roll64(p[1][2]))
+    gv_o[:, 128:192] = p[2][2][:, 0:64]
+
+    def unwindow(ref, res):
+        pieces = [ref[:, LANES * n : LANES * (n + 1)].astype(f32) for n in range(5)]
+        for n in range(5):
+            after = pieces[min(n + 1, 4)]
+            moved = jnp.where(low, roll64(pieces[n]), roll64(after))
+            value = jnp.where(first, pieces[n], moved)
+            if n < 4:
+                res[:, LANES * n : LANES * (n + 1)] = value
+            else:
+                res[:, 512:576] = value[:, 0:64]
+
+    unwindow(go, go_o)
+    unwindow(gd, gd_o)
+    for pair in range(4):
+        a, b = [
+            [ggu[2 * pair + odd, :, LANES * n : LANES * (n + 1)].astype(f32) for n in range(3)]
+            for odd in range(2)
+        ]
+        at = 384 * pair
+        gg_o[:, at : at + 128] = a[0]
+        gg_o[:, at + 128 : at + 256] = jnp.where(low, a[1], roll64(b[0]))
+        gg_o[:, at + 256 : at + 384] = jnp.where(low, roll64(b[0]), roll64(b[1]))
+        gu_o[:, at : at + 128] = a[2]
+        gu_o[:, at + 128 : at + 256] = jnp.where(low, roll64(a[1]), roll64(b[2]))
+        gu_o[:, at + 256 : at + 384] = jnp.where(low, roll64(b[2]), b[1])
+    ga_o[...] = small[0:1, 0:rows]
+    gf_o[...] = small[1:2, 0:rows]
+    width = out.shape[2]
+    rm_o[...] = jnp.sqrt(small[2:3, 0:3] / (small[2:3, 3:4] * width))
+
+
+def fast_device(
+    inputs,
+    segments,
+    weight_query,
+    key_weight_matrix,
+    value_weight_matrix,
+    weight_out,
+    weight_gate,
+    weight_up,
+    weight_down,
+    gain_attention,
+    gain_feed,
+    cotangent,
+):
+    f32, bf16 = jnp.float32, jnp.bfloat16
+    micro, _, rows, width = inputs.shape
+    dp = lax.axis_index("dp")
+    length = rows * 16
+    piece = width // 16
+
+    whole = pl.BlockSpec(memory_space=pltpu.VMEM)
+    meta, wq, wo, gu, wd = pl.pallas_call(
+        prepare_kernel,
+        out_shape=(
+            jax.ShapeDtypeStruct((8, LANES), f32),
+            jax.ShapeDtypeStruct((3, piece, 384), bf16),
+            jax.ShapeDtypeStruct((piece, 640), bf16),
+            jax.ShapeDtypeStruct((8, piece, 384), bf16),
+            jax.ShapeDtypeStruct((192, 640), bf16),
+        ),
+        in_specs=[whole] * 10,
+        out_specs=[whole] * 5,
+        name="prepare",
+    )(
+        gain_attention.reshape(1, piece),
+        gain_feed.reshape(1, piece),
+        segments[:, 0],
+        weight_query,
+        key_weight_matrix,
+        value_weight_matrix,
+        weight_out,
+        weight_gate,
+        weight_up,
+        weight_down,
+    )
+    half = HEAD_DIMENSION // 2
+    frequency = THETA ** (-np.arange(half, dtype=np.float32) * np.float32(2.0) / HEAD_DIMENSION)
+    angles = np.arange(length, dtype=np.float32)[:, None] * frequency.astype(np.float32)[None, :]
+    cosine, sine = np.cos(angles), np.sin(angles)
+    cosine = np.concatenate([cosine] * 4, axis=1).astype(np.float32)
+    sine = np.concatenate([-sine, sine, -sine, sine], axis=1).astype(np.float32)
+
+    v = pltpu.VMEM
+    tok = (2, 4, 2, 64, width)
+    scratch = [
+        v((16, 8, LANES), f32),
+        v((2, 64, width), bf16),
+        v((2, 64, width), bf16),
+        v(tok, bf16),
+        v(tok, bf16),
+        v(tok, bf16),
+        v((16, 72, 384), bf16),
+        v((width, 384), bf16),
+        v((2, 2, 4, 2, 72, 640), bf16),
+        v((width, width), bf16),
+        v((2, 2, 8, 72, 384), bf16),
+        v((2, width, 384), bf16),
+        v((2, 2, 192, 640), bf16),
+        v((2, 256, width), bf16),
+        v((width, 640), f32),
+        v((1024, 256), bf16),
+        v((192, 1024), bf16),
+        v((192, 1024), bf16),
+        v((3, 1024, 256), bf16),
+        v((3, 1024, 256), bf16),
+        v((3, 256, 256), bf16),
+        v((3, 256, 512), bf16),
+        v((3, 256, 768), bf16),
+        v((3, 256, 1024), bf16),
+        v((1024, 256), f32),
+        v((8, 1024), f32),
+        v((1024, 8), f32),
+        v((8, width), f32),
+        v((2, 8, 64, 256), bf16),
+        v((6, 2, 64, 256), bf16),
+        v((128, width), f32),
+        v((128, width), f32),
+        v((2, 2, 8, 64, 256), bf16),
+        v((2, 2, 8, 64, 384), bf16),
+        v((2, 4, 2, 64, width), bf16),
+        v((4, 2, 64, width), bf16),
+        v((3, 2, 64, width), bf16),
+        v((4, 2, 64, width), bf16),
+        v((3, 2, 64, width), bf16),
+        v((6, 2, 64, 256), bf16),
+        v((2, 8, 64, 256), bf16),
+        v((2, 8, 64, 384), bf16),
+        v((128, 1024), f32),
+        v((2, 8, 72, 384), bf16),
+        v((8, 72, 384), bf16),
+        v((8, 72, 384), bf16),
+        v((2, 2, 192, 640), bf16),
+        v((2, 192, 640), bf16),
+        v((192, 640), bf16),
+        v((2, 2, 4, 72, 640), bf16),
+        v((2, 72, 640), bf16),
+        v((3, 2, 2, 72, 640), bf16),
+        v((72, 640), bf16),
+        v((4, 3, 72, 384), bf16),
+        v((16, 8, LANES), f32),
+        v((32, 8, LANES), f32),
+        v((2, 2, 64, width), bf16),
+        v((2, 64, width), bf16),
+        pltpu.SemaphoreType.DMA((256,)),
+        pltpu.SemaphoreType.DMA((256,)),
+    ]
+    out, gin, gq, go, ggu, gd, small = pl.pallas_call(
+        fast_kernel,
+        out_shape=(
+            jax.ShapeDtypeStruct((2, rows, width), bf16),
+            jax.ShapeDtypeStruct((2, rows, width), bf16),
+            jax.ShapeDtypeStruct((3, piece, 384), f32),
+            jax.ShapeDtypeStruct((piece, 640), f32),
+            jax.ShapeDtypeStruct((8, piece, 384), bf16),
+            jax.ShapeDtypeStruct((192, 640), f32),
+            jax.ShapeDtypeStruct((8, LANES), f32),
+        ),
+        in_specs=[whole] * 9,
+        out_specs=[whole] * 7,
+        scratch_shapes=scratch,
+        compiler_params=pltpu.CompilerParams(
+            has_side_effects=True, vmem_limit_bytes=62 * 1024 * 1024
+        ),
+        name="layer",
+    )(
+        meta,
+        inputs[:, 0],
+        cotangent[:, 0],
+        wq,
+        wo,
+        gu,
+        wd,
+        jnp.asarray(cosine),
+        jnp.asarray(sine),
+    )
+
+    grads = pl.pallas_call(
+        finish_kernel,
+        out_shape=(
+            jax.ShapeDtypeStruct((2, rows, width), bf16),
+            jax.ShapeDtypeStruct((2, rows, width), bf16),
+            jax.ShapeDtypeStruct(weight_query.shape, f32),
+            jax.ShapeDtypeStruct(key_weight_matrix.shape, f32),
+            jax.ShapeDtypeStruct(value_weight_matrix.shape, f32),
+            jax.ShapeDtypeStruct(weight_out.shape, f32),
+            jax.ShapeDtypeStruct(weight_gate.shape, f32),
+            jax.ShapeDtypeStruct(weight_up.shape, f32),
+            jax.ShapeDtypeStruct(weight_down.shape, f32),
+            jax.ShapeDtypeStruct((1, piece), f32),
+            jax.ShapeDtypeStruct((1, piece), f32),
+            jax.ShapeDtypeStruct((1, 3), f32),
+        ),
+        in_specs=[whole] * 7,
+        out_specs=[whole] * 12,
+        name="finish",
+    )(out, gin, gq, go, ggu, gd, small)
+    return (
+        grads[0][:, None],
+        grads[1][:, None],
+        *grads[2:9],
+        grads[9].reshape(piece),
+        grads[10].reshape(piece),
+        grads[11].reshape(3),
+    )
+
+
 def solution(mesh):
     placed = (
         P(None, "dp", "seq", None),
@@ -528,8 +1862,9 @@
         P("seq"),
         P(None, "dp", "seq", None),
     )
+    body = fast_device if dict(mesh.shape) == {"dp": 2, "seq": 16} else per_device
     return jax.shard_map(
-        per_device,
+        body,
         mesh=mesh,
         in_specs=placed,
         out_specs=(

time: 1200 us -> 232 us (0.19)
  blocking collectives: 445 us -> 0 us
  waiting for transfers between devices: 403 us -> 0 us
  Pallas kernels: 0 us -> 231 us
  matrix products: 145 us -> 0 us
  local copies, waits for them, and re-layouts: 124 us -> 0 us
  other arithmetic: 50.4 us -> 0 us
  between operations: 23 us -> 0.81 us
    all_gather x17 -> x0, blocking collectives: 345 us -> none  [the longest x2 86.4 us: per_device(): lax.all_gather(log_total, 'seq', axis=3, tiled=True)]
    reduce_scatter x5 -> x0, waiting for transfers between devices: 262 us -> none  [the longest x3 233 us: reduce_grads(): lax.psum_scatter(g.astype(jnp.bfloat16), 'seq', scatter_dimension=0, tile...]
    pallas_call x0 -> x3, Pallas kernels: none -> 231 us  [the longest x1 225 us: fast_device(): pl.pallas_call(fast_kernel, out_shape=(jax.ShapeDtypeStruct((2, rows, wid...]
    dot_general x62 -> x0, matrix products: 145 us -> none  [the longest x14 41.4 us: weight_grad(): jnp.einsum('std,stf->df', acts_low, grads_low, preferred_element_type=jnp...]
    unnamed x32 -> x0, waiting for transfers between devices: 141 us -> none
    unnamed x1 -> x0, blocking collectives: 58.8 us -> none
    unnamed x282 -> x0, local copies, waits for them, and re-layouts: 44.9 us -> none
    psum x1 -> x0, blocking collectives: 40.5 us -> none  [per_device(): gain_total, totals = lax.psum((gain_grads, totals), ('dp', 'seq'))]
  transfers between devices with their start and end apart: 23 -> 0, of which waited for: 13 -> 0; matrix products, arithmetic and copies ran while one was open for 26% -> 0% of each run, Pallas kernels for 0% -> 0%
where the time goes in v2:
time: 232 us
  Pallas kernels  231 us (100%)
    pallas_call x1, Pallas kernels, fast_device(): pl.pallas_call(fast_kernel, out_shape=(jax.ShapeDtypeStruct((2, rows, wid...  225 us

profile of v2, /device:TPU:0, one launch (start us, length us, event | category | flops | bytes accessed | tf_op | source)
XLA Modules:
  0.0 231.7 jit_solution(2267611055482103527)
XLA Ops:
  0.6 2.6 %prepare.1 = (f32[8,128]{1,0:T(8,128)}, bf16[3,72,384]{2,1,0:T(8,128)(2,1)}, bf16[72,640]{1,0:T(8,128)(2,1)}, bf16[8,72,384]{2,1,0:T(8,128)(2,1)}, bf16[192,640]{1,0:T(8,128)(2,1)}) custom-call(bf16[1,72]{1,0:T(2,128)(2,1)} %bitcast.17, bf16[1,72]{1,0:T(2,128)(2,1)} %bitcast.18, s32[2,64]{1,0:T(2,128)} %bitcast.16, bf16[72,576]{1,0:T(8,128)(2,1)} %wq.1, ...), custom_call_target="tpu_custom_call" | custom-call | tf_op jit(solution)/shard_map/prepare/pallas_call | solution.py:1695
  3.2 225.1 %layer.1 = (bf16[2,64,1152]{2,1,0:T(8,128)(2,1)}, bf16[2,64,1152]{2,1,0:T(8,128)(2,1)}, f32[3,72,384]{2,1,0:T(8,128)}, f32[72,640]{1,0:T(8,128)}, bf16[8,72,384]...) custom-call(f32[8,128]{1,0:T(8,128)} %get-tuple-element.36.meta_in, bf16[2,64,1152]{2,1,0:T(8,128)(2,1)} %bitcast.14, ...), custom_call_target="tpu_custom_call" | custom-call | tf_op jit(solution)/shard_map/layer/pallas_call | solution.py:1790
  228.3 3.2 %finish.1 = (bf16[2,64,1152]{2,1,0:T(8,128)(2,1)}, bf16[2,64,1152]{2,1,0:T(8,128)(2,1)}, f32[72,576]{1,0:T(8,128)}, f32[72,192]{1,0:T(8,128)}, f32[72,192]{1,0:T...) custom-call(bf16[2,64,1152]{2,1,0:T(8,128)(2,1)} %get-tuple-element., ...), custom_call_target="tpu_custom_call" | custom-call | tf_op jit(solution)/shard_map/finish/pallas_call | solution.py:1820

commit v3 on v2

--- a/solution.py
+++ b/solution.py
@@ -520,16 +520,88 @@
 LANES = 128
 
 
+def roll64(values):
+    return pltpu.roll(values, 64, 1)
+
+
+def prepare(
+    ga, gf, seg, wq, wk, wv, wo, gate, up, wd, meta_o, wq_o, wo_o, gu_o, wd_o
+):
+    f32, bf16 = jnp.float32, jnp.bfloat16
+    first = lax.axis_index("dp") == 0
+    rows = wq.shape[0]
+    low = lax.broadcasted_iota(jnp.int32, (1, LANES), 1) < 64
+    meta_o[...] = jnp.zeros(meta_o.shape, f32)
+    meta_o[0:1, 0:rows] = ga[...].astype(f32)
+    meta_o[1:2, 0:rows] = gf[...].astype(f32)
+    meta_o[2:4, 0:64] = seg[...].astype(f32)
+
+    def part(ref, at, size=LANES):
+        values = ref[:, at : at + size].astype(f32)
+        if size < LANES:
+            values = jnp.concatenate(
+                [values, jnp.zeros((values.shape[0], LANES - size), f32)], axis=1
+            )
+        return values
+
+    q = [part(wq, LANES * n) for n in range(4)] + [part(wq, 512, 64)]
+    k = [part(wk, 0), part(wk, LANES, 64)]
+    v = [part(wv, 0), part(wv, LANES, 64)]
+    slabs = (
+        (q[0], jnp.where(low, q[1], roll64(k[0])), jnp.where(low, v[0], 0.0)),
+        (
+            jnp.where(low, roll64(q[1]), roll64(q[2])),
+            jnp.where(low, roll64(q[2]), k[0]),
+            jnp.where(low, roll64(v[0]), 0.0),
+        ),
+        (q[3], jnp.where(low, q[4], roll64(k[1])), v[1]),
+    )
+    for head in range(3):
+        for place in range(3):
+            wq_o[head, :, LANES * place : LANES * (place + 1)] = slabs[head][place].astype(bf16)
+
+    def window(ref, out):
+        pieces = [part(ref, LANES * n) for n in range(4)] + [part(ref, 512, 64)]
+        before = jnp.zeros_like(pieces[0])
+        for n in range(5):
+            moved = jnp.where(low, roll64(before), roll64(pieces[n]))
+            out[:, LANES * n : LANES * (n + 1)] = jnp.where(first, pieces[n], moved).astype(bf16)
+            before = pieces[n]
+
+    window(wo, wo_o)
+    window(wd, wd_o)
+    for pair in range(4):
+        g = [part(gate, 384 * pair + LANES * n) for n in range(3)]
+        u = [part(up, 384 * pair + LANES * n) for n in range(3)]
+        slabs = (
+            (g[0], jnp.where(low, g[1], roll64(u[1])), u[0]),
+            (
+                jnp.where(low, roll64(g[1]), roll64(g[2])),
+                jnp.where(low, roll64(g[2]), u[2]),
+                jnp.where(low, roll64(u[1]), roll64(u[2])),
+            ),
+        )
+        for odd in range(2):
+            for place in range(3):
+                gu_o[2 * pair + odd, :, LANES * place : LANES * (place + 1)] = slabs[odd][
+                    place
+                ].astype(bf16)
+
+
 def fast_kernel(
-    meta_in,
     x_in,
     cot_in,
-    wq_in,
-    wo_in,
-    gu_in,
-    wd_in,
-    cos_in,
-    sin_in,
+    ga,
+    gf,
+    seg,
+    wq,
+    wk,
+    wv,
+    wo,
+    gate,
+    up,
+    wd,
+    turn_in,
     out_o,
     gin_o,
     gq_o,
@@ -537,6 +609,9 @@
     ggu_o,
     gd_o,
     small_o,
+    meta_in,
+    wq_in,
+    wo_in,
     meta_r,
     xo,
     co,
@@ -600,6 +675,7 @@
 ):
     f32, bf16 = jnp.float32, jnp.bfloat16
     part_f = n2g
+    gu_in, wd_in = guf_r, gd_s.at[0, 0]
     e1r1, e1r2 = gfg.at[0], gfg.at[1]
     x = lax.axis_index("dp")
     s = lax.axis_index("seq")
@@ -615,6 +691,17 @@
     head_own = head_of(j)
     width = x_in.shape[2]
     counter = [0]
+    everyone = pltpu.get_barrier_semaphore()
+    for other in range(1, 32):
+        there = (x * 16 + s + other) % 32
+        pl.semaphore_signal(
+            everyone,
+            inc=1,
+            device_id=(there // 16, there % 16),
+            device_id_type=pl.DeviceIdType.MESH,
+        )
+    prepare(ga, gf, seg, wq, wk, wv, wo, gate, up, wd, meta_in, wq_in, wo_in, gu_in, wd_in)
+    pl.semaphore_wait(everyone, 31)
     pending = []
 
     def index_of(mask):
@@ -716,7 +803,7 @@
         return lambda chip: n1g.at[half, chip, c]
 
     x_a = Gather(tokens_of(zh), True, (True, False))
-    x_b = Gather(tokens_of(1 - zh), True, (False, True))
+    x_b = Gather(tokens_of(1 - zh), True, (True, False))
     x_a.start(x_in.at[zh])
     x_copy = send(x_in.at[1 - zh], n1g.at[zh, own_chip, c], device(0, False, True))
     meta_copies = []
@@ -860,8 +947,10 @@
         return jnp.where(low_half, pltpu.roll(values, 256 - 32, 1), pltpu.roll(values, 32, 1))
 
     def tables(at, rows):
-        cosine = cos_in[pl.ds(at, rows), :]
-        sine = sin_in[pl.ds(at, rows), :]
+        both = turn_in[pl.ds(at, rows), :]
+        first_half = lane256[:, 0:128] < 64
+        cosine = jnp.where(first_half, both, roll64(both))
+        sine = jnp.where(first_half, roll64(both), both)
         return (
             jnp.concatenate([cosine, cosine], axis=1),
             jnp.concatenate([sine, sine], axis=1),
@@ -934,6 +1023,7 @@
     pl.when(attends)(lambda: attend_block(1))
     for copy in gu_first:
         copy.wait_recv()
+        copy.wait_send()
     gu_z = []
     for part in range(2):
         rows = gu_r.at[x, zh, 4 * part : 4 * part + 4]
@@ -1194,6 +1284,9 @@
         from_rows(cut)
     ggu_x = send(gu_r.at[1 - x], gux_r, device(0, True))
 
+    wd_z.wait_send()
+    wd_x.wait_send()
+
     def down_step(chunk, carry):
         grads = gfg[...].reshape(1024, width)
         piece = mm_w(inner_s[chunk].reshape(1024, 256), grads)
@@ -1526,7 +1619,7 @@
     ret_in.wait_recv()
     gin_o[1 - zh] = rows_r[1]
 
-    waited = {id(copy) for copy in wo_c + wo_x + gu_x + gu_z}
+    waited = {id(copy) for copy in wo_c + wo_x + gu_x + gu_z + gu_first + [wd_z, wd_x]}
     for gather in (wo_q, gf_all, n2_all, x_a, x_b):
         waited |= {id(copy) for copy in gather.copies}
     for copy in pending:
@@ -1549,74 +1642,6 @@
             return carry
 
         lax.fori_loop(0, 16, step, 0)
-
-
-def roll64(values):
-    return pltpu.roll(values, 64, 1)
-
-
-def prepare_kernel(
-    ga, gf, seg, wq, wk, wv, wo, gate, up, wd, meta_o, wq_o, wo_o, gu_o, wd_o
-):
-    f32, bf16 = jnp.float32, jnp.bfloat16
-    first = lax.axis_index("dp") == 0
-    rows = wq.shape[0]
-    low = lax.broadcasted_iota(jnp.int32, (1, LANES), 1) < 64
-    meta_o[...] = jnp.zeros(meta_o.shape, f32)
-    meta_o[0:1, 0:rows] = ga[...].astype(f32)
-    meta_o[1:2, 0:rows] = gf[...].astype(f32)
-    meta_o[2:4, 0:64] = seg[...].astype(f32)
-
-    def part(ref, at, size=LANES):
-        values = ref[:, at : at + size].astype(f32)
-        if size < LANES:
-            values = jnp.concatenate(
-                [values, jnp.zeros((values.shape[0], LANES - size), f32)], axis=1
-            )
-        return values
-
-    q = [part(wq, LANES * n) for n in range(4)] + [part(wq, 512, 64)]
-    k = [part(wk, 0), part(wk, LANES, 64)]
-    v = [part(wv, 0), part(wv, LANES, 64)]
-    slabs = (
-        (q[0], jnp.where(low, q[1], roll64(k[0])), jnp.where(low, v[0], 0.0)),
-        (
-            jnp.where(low, roll64(q[1]), roll64(q[2])),
-            jnp.where(low, roll64(q[2]), k[0]),
-            jnp.where(low, roll64(v[0]), 0.0),
-        ),
-        (q[3], jnp.where(low, q[4], roll64(k[1])), v[1]),
-    )
-    for head in range(3):
-        for place in range(3):
-            wq_o[head, :, LANES * place : LANES * (place + 1)] = slabs[head][place].astype(bf16)
-
-    def window(ref, out):
-        pieces = [part(ref, LANES * n) for n in range(4)] + [part(ref, 512, 64)]
-        before = jnp.zeros_like(pieces[0])
-        for n in range(5):
-            moved = jnp.where(low, roll64(before), roll64(pieces[n]))
-            out[:, LANES * n : LANES * (n + 1)] = jnp.where(first, pieces[n], moved).astype(bf16)
-            before = pieces[n]
-
-    window(wo, wo_o)
-    window(wd, wd_o)
-    for pair in range(4):
-        g = [part(gate, 384 * pair + LANES * n) for n in range(3)]
-        u = [part(up, 384 * pair + LANES * n) for n in range(3)]
-        slabs = (
-            (g[0], jnp.where(low, g[1], roll64(u[1])), u[0]),
-            (
-                jnp.where(low, roll64(g[1]), roll64(g[2])),
-                jnp.where(low, roll64(g[2]), u[2]),
-                jnp.where(low, roll64(u[1]), roll64(u[2])),
-            ),
-        )
-        for odd in range(2):
-            for place in range(3):
-                gu_o[2 * pair + odd, :, LANES * place : LANES * (place + 1)] = slabs[odd][
-                    place
-                ].astype(bf16)
 
 
 def finish_kernel(
@@ -1692,40 +1717,18 @@
     piece = width // 16
 
     whole = pl.BlockSpec(memory_space=pltpu.VMEM)
-    meta, wq, wo, gu, wd = pl.pallas_call(
-        prepare_kernel,
-        out_shape=(
-            jax.ShapeDtypeStruct((8, LANES), f32),
-            jax.ShapeDtypeStruct((3, piece, 384), bf16),
-            jax.ShapeDtypeStruct((piece, 640), bf16),
-            jax.ShapeDtypeStruct((8, piece, 384), bf16),
-            jax.ShapeDtypeStruct((192, 640), bf16),
-        ),
-        in_specs=[whole] * 10,
-        out_specs=[whole] * 5,
-        name="prepare",
-    )(
-        gain_attention.reshape(1, piece),
-        gain_feed.reshape(1, piece),
-        segments[:, 0],
-        weight_query,
-        key_weight_matrix,
-        value_weight_matrix,
-        weight_out,
-        weight_gate,
-        weight_up,
-        weight_down,
-    )
     half = HEAD_DIMENSION // 2
     frequency = THETA ** (-np.arange(half, dtype=np.float32) * np.float32(2.0) / HEAD_DIMENSION)
     angles = np.arange(length, dtype=np.float32)[:, None] * frequency.astype(np.float32)[None, :]
     cosine, sine = np.cos(angles), np.sin(angles)
-    cosine = np.concatenate([cosine] * 4, axis=1).astype(np.float32)
-    sine = np.concatenate([-sine, sine, -sine, sine], axis=1).astype(np.float32)
+    turns = np.concatenate([cosine, cosine, -sine, sine], axis=1).astype(np.float32)
 
     v = pltpu.VMEM
     tok = (2, 4, 2, 64, width)
     scratch = [
+        v((8, LANES), f32),
+        v((3, piece, 384), bf16),
+        v((piece, 640), bf16),
         v((16, 8, LANES), f32),
         v((2, 64, width), bf16),
         v((2, 64, width), bf16),
@@ -1798,23 +1801,27 @@
             jax.ShapeDtypeStruct((192, 640), f32),
             jax.ShapeDtypeStruct((8, LANES), f32),
         ),
-        in_specs=[whole] * 9,
+        in_specs=[whole] * 13,
         out_specs=[whole] * 7,
         scratch_shapes=scratch,
         compiler_params=pltpu.CompilerParams(
-            has_side_effects=True, vmem_limit_bytes=62 * 1024 * 1024
+            has_side_effects=True, collective_id=0, vmem_limit_bytes=62 * 1024 * 1024
         ),
         name="layer",
     )(
-        meta,
         inputs[:, 0],
         cotangent[:, 0],
-        wq,
-        wo,
-        gu,
-        wd,
-        jnp.asarray(cosine),
-        jnp.asarray(sine),
+        gain_attention.reshape(1, piece),
+        gain_feed.reshape(1, piece),
+        segments[:, 0],
+        weight_query,
+        key_weight_matrix,
+        value_weight_matrix,
+        weight_out,
+        weight_gate,
+        weight_up,
+        weight_down,
+        jnp.asarray(turns),
     )
 
     grads = pl.pallas_call(

time: 232 us -> 223 us (0.961)
  Pallas kernels: 231 us -> 221 us
    pallas_call x1, Pallas kernels: 225 us -> 218 us  [fast_device(): pl.pallas_call(fast_kernel, out_shape=(jax.ShapeDtypeStruct((2, rows, wid...]
    pallas_call x1 -> x0, Pallas kernels: 2.58 us -> none  [fast_device(): pl.pallas_call(prepare_kernel, out_shape=(jax.ShapeDtypeStruct((8, LANES)...]
where the time goes in v3:
time: 223 us; the launch traced here: 222 us
  Pallas kernels  221 us (99%)
    pallas_call x1, Pallas kernels, fast_device(): pl.pallas_call(fast_kernel, out_shape=(jax.ShapeDtypeStruct((2, rows, wid...  218 us

profile of v3, /device:TPU:0, one launch (start us, length us, event | category | flops | bytes accessed | tf_op | source)
XLA Modules:
  0.0 222.2 jit_solution(2877050272829503321)
XLA Ops:
  0.6 218.1 %layer.1 = (bf16[2,64,1152]{2,1,0:T(8,128)(2,1)}, bf16[2,64,1152]{2,1,0:T(8,128)(2,1)}, f32[3,72,384]{2,1,0:T(8,128)}, f32[72,640]{1,0:T(8,128)}, bf16[8,72,384]...) custom-call(bf16[2,64,1152]{2,1,0:T(8,128)(2,1)} %bitcast.14, bf16[2,64,1152]{2,1,0:T(8,128)(2,1)} %bitcast.15, ...), custom_call_target="tpu_custom_call" | custom-call | tf_op jit(solution)/shard_map/layer/pallas_call | solution.py:1793
  218.8 3.2 %finish.1 = (bf16[2,64,1152]{2,1,0:T(8,128)(2,1)}, bf16[2,64,1152]{2,1,0:T(8,128)(2,1)}, f32[72,576]{1,0:T(8,128)}, f32[72,192]{1,0:T(8,128)}, f32[72,192]{1,0:T...) custom-call(bf16[2,64,1152]{2,1,0:T(8,128)(2,1)} %get-tuple-element., ...), custom_call_target="tpu_custom_call" | custom-call | tf_op jit(solution)/shard_map/finish/pallas_call | solution.py:1827

commit v4 on v3

--- a/solution.py
+++ b/solution.py
@@ -1184,7 +1184,7 @@
         for kind in ((0, 1), (2,), (3,))[step]:
             side_copy(ref, got2, base, kind).start()
 
-    def scatter_first(ref, got, got2, compute):
+    def scatter_first(ref, got, got2, compute, sides=True):
         base = counter[0]
         counter[0] += 10
 
@@ -1193,7 +1193,7 @@
             block = compute(chip).astype(bf16).reshape(2, 2, 64, width)
             ref[:, chip] = block
             pair_copy(ref, got, base, step).start()
-            for done in range(3):
+            for done in range(3 if sides else 0):
                 pl.when(step == done + 1)(
                     functools.partial(scatter_side, ref, got, got2, base, done)
                 )
@@ -1304,7 +1304,7 @@
         return total + mm(inner_s[1, :, pl.ds(chip * 2, 2)].reshape(256, 256), wd_w[1])
 
     n2_all.sent()
-    bf_base = scatter_first(part_f, bfr1, bfr2, result_block)
+    bf_base = scatter_first(part_f, bfr1, bfr2, result_block, False)
 
     e2 = scatter_finish(part_e, e2r1, e2r2, e2_base)
     hidden = hid[...]
@@ -1341,6 +1341,8 @@
     def _():
         da_r[:, j] = da_s[head_own]
 
+    for step in range(3):
+        scatter_side(part_f, bfr1, bfr2, bf_base, step)
     for copy in wo_c + wo_x:
         copy.wait_send()
     wo_q.sent()
@@ -1469,6 +1471,47 @@
 
     scatter_sent(part_e, e2r1, e2r2, e2_base)
     e1_base = scatter_first(part_e, e1r1, e1r2, input_block)
+    gq_send, gq_sem = fresh(), fresh()
+    plane_to = zl
+    piece_own = head_own - 3 * zl
+
+    def gq_copy(slot):
+        return pltpu.make_async_remote_copy(
+            src_ref=wq_r.at[slot],
+            dst_ref=gq_r.at[x * 2 + zh, piece_own],
+            send_sem=ssem.at[gq_send],
+            recv_sem=rsem.at[gq_sem],
+            device_id=(plane_to, slot),
+            device_id_type=pl.DeviceIdType.MESH,
+        )
+
+    @pl.when(attends)
+    def _():
+        grads = d_s[...].reshape(1024, 384)
+
+        def wide_step(block, carry):
+            at = pl.multiple_of(block * 128, 128)
+            rows = n1g[:, :, :, :, pl.ds(at, 128)].reshape(1024, 128)
+            acc[pl.ds(at, 128), 0:384] = mm_w(rows, grads)
+            return carry
+
+        lax.fori_loop(0, 9, wide_step, 0)
+
+        def step(slot, carry):
+            wq_r[slot] = acc[pl.ds(pl.multiple_of(slot * 72, 8), 72), 0:384].astype(bf16)
+            here = (plane_to == x) & (slot == s)
+
+            @pl.when(here)
+            def _():
+                pltpu.make_async_copy(
+                    wq_r.at[slot], gq_r.at[x * 2 + zh, piece_own], rsem.at[gq_sem]
+                ).start()
+
+            pl.when(jnp.logical_not(here))(lambda: gq_copy(slot).start())
+            return carry
+
+        lax.fori_loop(0, 16, step, 0)
+
     scatter_second(part_e, e1r1, e1r2, e1_base)
 
     ggd_x.wait_recv()
@@ -1492,47 +1535,6 @@
     ret_out = send(rows_s.at[0, 1 - zh], rows_r.at[0], device(0, False, True))
     out_o[zh] = rows_s[0, zh]
 
-    gq_send, gq_sem = fresh(), fresh()
-    plane_to = zl
-    piece_own = head_own - 3 * zl
-
-    def gq_copy(slot):
-        return pltpu.make_async_remote_copy(
-            src_ref=wq_r.at[slot],
-            dst_ref=gq_r.at[x * 2 + zh, piece_own],
-            send_sem=ssem.at[gq_send],
-            recv_sem=rsem.at[gq_sem],
-            device_id=(plane_to, slot),
-            device_id_type=pl.DeviceIdType.MESH,
-        )
-
-    @pl.when(attends)
-    def _():
-        grads = d_s[...].reshape(1024, 384)
-
-        def wide_step(block, carry):
-            at = pl.multiple_of(block * 128, 128)
-            rows = n1g[:, :, :, :, pl.ds(at, 128)].reshape(1024, 128)
-            acc[pl.ds(at, 128), 0:384] = mm_w(rows, grads)
-            return carry
-
-        lax.fori_loop(0, 9, wide_step, 0)
-
-        def step(slot, carry):
-            wq_r[slot] = acc[pl.ds(pl.multiple_of(slot * 72, 8), 72), 0:384].astype(bf16)
-            here = (plane_to == x) & (slot == s)
-
-            @pl.when(here)
-            def _():
-                pltpu.make_async_copy(
-                    wq_r.at[slot], gq_r.at[x * 2 + zh, piece_own], rsem.at[gq_sem]
-                ).start()
-
-            pl.when(jnp.logical_not(here))(lambda: gq_copy(slot).start())
-            return carry
-
-        lax.fori_loop(0, 16, step, 0)
-
     ggu_z.wait_recv()
 
     def gu_add2(slot, carry):
@@ -1542,10 +1544,6 @@
         return carry
 
     lax.fori_loop(0, 8, gu_add2, 0)
-    ggu_q = [
-        send(gu_r.at[x, zh, index_of(mask)], guf_r.at[j], device(mask)) for mask in range(1, 8)
-    ]
-    guf_r[j] = gu_r[x, zh, j]
     e1 = scatter_finish(part_e, e1r1, e1r2, e1_base)
     tokens = xo[...].reshape(128, width).astype(f32)
     scale1 = lax.rsqrt(jnp.mean(tokens * tokens, axis=-1, keepdims=True) + EPS)
@@ -1559,6 +1557,10 @@
     ret_in = send(rows_s.at[1, 1 - zh], rows_r.at[1], device(0, False, True))
     gin_o[zh] = rows_s[1, zh]
 
+    ggu_q = [
+        send(gu_r.at[x, zh, index_of(mask)], guf_r.at[j], device(mask)) for mask in range(1, 8)
+    ]
+    guf_r[j] = gu_r[x, zh, j]
     total_row = jnp.where(
         lane1 == 0,
         square_attn,

time: 223 us -> 220 us (0.987)
    pallas_call x1, Pallas kernels: 218 us -> 216 us  [fast_device(): pl.pallas_call(fast_kernel, out_shape=(jax.ShapeDtypeStruct((2, rows, wid...]
where the time goes in v4:
time: 220 us
  Pallas kernels  219 us (100%)
    pallas_call x1, Pallas kernels, fast_device(): pl.pallas_call(fast_kernel, out_shape=(jax.ShapeDtypeStruct((2, rows, wid...  216 us

profile of v4, /device:TPU:0, one launch (start us, length us, event | category | flops | bytes accessed | tf_op | source)
XLA Modules:
  0.0 219.7 jit_solution(1289458161492616315)
XLA Ops:
  0.6 215.6 %layer.1 = (bf16[2,64,1152]{2,1,0:T(8,128)(2,1)}, bf16[2,64,1152]{2,1,0:T(8,128)(2,1)}, f32[3,72,384]{2,1,0:T(8,128)}, f32[72,640]{1,0:T(8,128)}, bf16[8,72,384]...) custom-call(bf16[2,64,1152]{2,1,0:T(8,128)(2,1)} %bitcast.14, bf16[2,64,1152]{2,1,0:T(8,128)(2,1)} %bitcast.15, ...), custom_call_target="tpu_custom_call" | custom-call | tf_op jit(solution)/shard_map/layer/pallas_call | solution.py:1795
  216.3 3.2 %finish.1 = (bf16[2,64,1152]{2,1,0:T(8,128)(2,1)}, bf16[2,64,1152]{2,1,0:T(8,128)(2,1)}, f32[72,576]{1,0:T(8,128)}, f32[72,192]{1,0:T(8,128)}, f32[72,192]{1,0:T...) custom-call(bf16[2,64,1152]{2,1,0:T(8,128)(2,1)} %get-tuple-element., ...), custom_call_target="tpu_custom_call" | custom-call | tf_op jit(solution)/shard_map/finish/pallas_call | solution.py:1829

commit v5 on v4

--- a/solution.py
+++ b/solution.py
@@ -1036,7 +1036,7 @@
     pl.when(attends)(lambda: attend_block(3))
 
     at_copies = []
-    for mask in range(1, 8):
+    for mask in (6, 7, 4, 5, 2, 3, 1):
         n = fresh()
         there = index_of(mask)
         copy = pltpu.make_async_remote_copy(
@@ -1323,7 +1323,7 @@
         piece = mm_t(d_low, wo_w[192 * head : 192 * head + 192, :])
         da_s[head, :, :, 0:192] = piece.astype(bf16).reshape(2, 64, 192)
     da_copies = []
-    for mask in range(1, 8):
+    for mask in (6, 7, 4, 5, 2, 3, 1):
         n = fresh()
         there = index_of(mask)
         copy = pltpu.make_async_remote_copy(
@@ -1576,9 +1576,9 @@
         moved = pltpu.roll(both_gains, (width - 72 * slot) % width, 1) if slot else both_gains
         small_s[slot] = jnp.where(row8 == 2, total_row, moved[:, 0:LANES])
     small_copies = []
-    for flip_x in (False, True):
-        for flip_z in (False, True):
-            for mask in range(8):
+    for flip_z in (True, False):
+        for flip_x in (True, False):
+            for mask in (6, 7, 4, 5, 2, 3, 1, 0):
                 if flip_x or flip_z or mask:
                     target = device(mask, flip_x, flip_z)
                     small_copies.append(

time: 220 us -> 219 us (level)
  no operation moved by 1% of the time
where the time goes in v5:
time: 219 us; the launch traced here: 218 us
  Pallas kernels  218 us (100%)
    pallas_call x1, Pallas kernels, fast_device(): pl.pallas_call(fast_kernel, out_shape=(jax.ShapeDtypeStruct((2, rows, wid...  214 us

profile of v5, /device:TPU:0, one launch (start us, length us, event | category | flops | bytes accessed | tf_op | source)
XLA Modules:
  0.0 218.4 jit_solution(6935727362718498131)
XLA Ops:
  0.6 214.4 %layer.1 = (bf16[2,64,1152]{2,1,0:T(8,128)(2,1)}, bf16[2,64,1152]{2,1,0:T(8,128)(2,1)}, f32[3,72,384]{2,1,0:T(8,128)}, f32[72,640]{1,0:T(8,128)}, bf16[8,72,384]...) custom-call(bf16[2,64,1152]{2,1,0:T(8,128)(2,1)} %bitcast.14, bf16[2,64,1152]{2,1,0:T(8,128)(2,1)} %bitcast.15, ...), custom_call_target="tpu_custom_call" | custom-call | tf_op jit(solution)/shard_map/layer/pallas_call | solution.py:1795
  215.0 3.2 %finish.1 = (bf16[2,64,1152]{2,1,0:T(8,128)(2,1)}, bf16[2,64,1152]{2,1,0:T(8,128)(2,1)}, f32[72,576]{1,0:T(8,128)}, f32[72,192]{1,0:T(8,128)}, f32[72,192]{1,0:T...) custom-call(bf16[2,64,1152]{2,1,0:T(8,128)(2,1)} %get-tuple-element., ...), custom_call_target="tpu_custom_call" | custom-call | tf_op jit(solution)/shard_map/finish/pallas_call | solution.py:1829

commit v6 on v5

--- a/solution.py
+++ b/solution.py
@@ -804,8 +804,8 @@
 
     x_a = Gather(tokens_of(zh), True, (True, False))
     x_b = Gather(tokens_of(1 - zh), True, (True, False))
+    x_copy = send(x_in.at[1 - zh], n1g.at[zh, own_chip, c], device(0, False, True))
     x_a.start(x_in.at[zh])
-    x_copy = send(x_in.at[1 - zh], n1g.at[zh, own_chip, c], device(0, False, True))
     meta_copies = []
     for mask in range(8):
         for far in (False, True):
@@ -1003,7 +1003,7 @@
                 scores = jnp.where(allowed, scores * scale, NEGATIVE)
                 top = jnp.max(scores, axis=-1, keepdims=True)
                 weight = jnp.exp(scores - top)
-                weight = weight / jnp.sum(weight, axis=-1, keepdims=True)
+                weight = weight * (1.0 / jnp.sum(weight, axis=-1, keepdims=True))
                 low_p = weight.astype(bf16)
                 pbs[quarter][head, pl.ds(pl.multiple_of(sub * 128, 128), 128), :] = low_p
                 mixed = mixed + mm(low_p, vw[head, 0:length, :])

time: 219 us -> 218 us (level)
  no operation moved by 1% of the time
where the time goes in v6:
time: 218 us
  Pallas kernels  217 us (100%)
    pallas_call x1, Pallas kernels, fast_device(): pl.pallas_call(fast_kernel, out_shape=(jax.ShapeDtypeStruct((2, rows, wid...  214 us

profile of v6, /device:TPU:0, one launch (start us, length us, event | category | flops | bytes accessed | tf_op | source)
XLA Modules:
  0.0 218.1 jit_solution(4337263296913897053)
XLA Ops:
  0.6 214.0 %layer.1 = (bf16[2,64,1152]{2,1,0:T(8,128)(2,1)}, bf16[2,64,1152]{2,1,0:T(8,128)(2,1)}, f32[3,72,384]{2,1,0:T(8,128)}, f32[72,640]{1,0:T(8,128)}, bf16[8,72,384]...) custom-call(bf16[2,64,1152]{2,1,0:T(8,128)(2,1)} %bitcast.14, bf16[2,64,1152]{2,1,0:T(8,128)(2,1)} %bitcast.15, ...), custom_call_target="tpu_custom_call" | custom-call | tf_op jit(solution)/shard_map/layer/pallas_call | solution.py:1795
  214.7 3.2 %finish.1 = (bf16[2,64,1152]{2,1,0:T(8,128)(2,1)}, bf16[2,64,1152]{2,1,0:T(8,128)(2,1)}, f32[72,576]{1,0:T(8,128)}, f32[72,192]{1,0:T(8,128)}, f32[72,192]{1,0:T...) custom-call(bf16[2,64,1152]{2,1,0:T(8,128)(2,1)} %get-tuple-element., ...), custom_call_target="tpu_custom_call" | custom-call | tf_op jit(solution)/shard_map/finish/pallas_call | solution.py:1829
